TPU v7x, 512 devices: a whole 4x4x16 slice. The times are simulated.
512 devices in a mesh: freq: 32 (over z, x_hi), sky: 16 (over y, x_lo, core).
Axes of the slice: x: 4 (x_hi: 2, x_lo: 2; x = x_hi * 2 + x_lo), y: 4, z: 16, core: 2. Of those that a mesh axis runs over, the one named last changes fastest.
Arguments:
- sky_cube: bfloat16 [64, 32, 2048], P('freq', 'sky'), may hold values from -24 to 24
- free_mask: int32 [64], P('freq'), may hold values 0 or 1
- conv_first: bfloat16 [32, 1, 3, 3, 3], replicated, may hold values from -1.25 to 1.25
- conv_second: bfloat16 [32, 32, 3, 3, 3], replicated, may hold values from -0.21875 to 0.21875
- proposal_conv: bfloat16 [3, 3, 64, 256], replicated, may hold values from -0.25 to 0.25
- score_head: bfloat16 [9, 256], replicated, may hold values from -0.375 to 0.375
- box_head: bfloat16 [36, 256], replicated, may hold values from -0.375 to 0.375
Outputs:
- objectness: float32 [9, 32, 2048], P(None, 'sky', 'freq')
- proposals: float32 [9, 4, 32, 2048], P(None, None, 'sky', 'freq')
All inputs are finite; a program needn't handle non-finite values. No bound on the sum of `free_mask` on one device may be relied on, other than what follows from the above.
Results may differ from a plain program's by a relative error of at most 0.0055.
Values may be sent and summed in bfloat16 or wider, within the bound.
A program may use at most 64 MiB of HBM per device.

v0:
```python
import jax
import jax.numpy as jnp
from jax import lax
from jax.sharding import PartitionSpec as P


def padded_2(block, sides, width):
    for axis, dim in sides:
        count = lax.axis_size(axis)
        forward = [(i, i + 1) for i in range(count - 1)]
        backward = [(target, source) for source, target in forward]
        low = lax.ppermute(
            lax.slice_in_dim(block, block.shape[dim] - width, None, axis=dim), axis, forward
        )
        high = lax.ppermute(lax.slice_in_dim(block, 0, width, axis=dim), axis, backward)
        block = jnp.concatenate([low, block, high], axis=dim)
    return block


def conv_volume(volume, kernel, paddings):
    return lax.conv_general_dilated(
        volume,
        kernel,
        (1, 1, 1),
        paddings,
        dimension_numbers=("NCDHW", "OIDHW", "NCDHW"),
        preferred_element_type=jnp.float32,
    )


def project_moments(second_layer, velocity, channel_total):
    zeroth = jnp.sum(second_layer, axis=1) / channel_total
    first_moment = jnp.einsum(
        "cnyx,n->cyx", second_layer, velocity, precision=lax.Precision.HIGHEST
    ) * (12.0 / channel_total)
    return jnp.concatenate([zeroth, first_moment], axis=0)


def decode_boxes(box_delta, row_start, col_start):
    anchor_count = box_delta.shape[0]
    map_height = box_delta.shape[2]
    map_width = box_delta.shape[3]
    anchor_index = jnp.arange(anchor_count, dtype=jnp.int32)
    anchor_scale = 4.0 * 2.0 ** (anchor_index // 3).astype(jnp.float32)
    anchor_ratio = 2.0 ** (anchor_index % 3 - 1).astype(jnp.float32)
    anchor_width = (anchor_scale * jnp.sqrt(anchor_ratio))[:, None, None]
    anchor_height = (anchor_scale / jnp.sqrt(anchor_ratio))[:, None, None]
    centre_rows = (row_start + jnp.arange(map_height, dtype=jnp.int32)).astype(jnp.float32) + 0.5
    centre_cols = (col_start + jnp.arange(map_width, dtype=jnp.int32)).astype(jnp.float32) + 0.5
    centre_x = centre_cols[None, None, :] + box_delta[:, 0] * anchor_width
    centre_y = centre_rows[None, :, None] + box_delta[:, 1] * anchor_height
    box_width = anchor_width * jnp.exp(box_delta[:, 2])
    box_height = anchor_height * jnp.exp(box_delta[:, 3])
    corners = jnp.stack(
        [
            centre_x - 0.5 * box_width,
            centre_y - 0.5 * box_height,
            centre_x + 0.5 * box_width,
            centre_y + 0.5 * box_height,
        ],
        axis=1,
    )
    return corners / 64.0


def propose(framed, proposal_conv, score_head, box_head, row_start, col_start):
    hidden = lax.conv_general_dilated(
        framed[None],
        proposal_conv,
        (1, 1),
        [(0, 0), (0, 0)],
        dimension_numbers=("NCHW", "HWIO", "NCHW"),
        preferred_element_type=jnp.float32,
    )
    hidden = jax.nn.relu(hidden[0]).astype(jnp.bfloat16)
    objectness = jnp.einsum("kc,cyx->kyx", score_head, hidden, preferred_element_type=jnp.float32)
    box_delta = jnp.einsum("kc,cyx->kyx", box_head, hidden, preferred_element_type=jnp.float32)
    box_delta = box_delta.reshape(score_head.shape[0], 4, hidden.shape[1], hidden.shape[2])
    return (objectness, decode_boxes(box_delta, row_start, col_start))


def on_device(sky_cube, free_mask, conv_first, conv_second, proposal_conv, score_head, box_head):
    freq_count = lax.axis_size("freq")
    freq_pos = lax.axis_index("freq")
    sky_pos = lax.axis_index("sky")
    chan_count = sky_cube.shape[0]
    row_count = sky_cube.shape[1]
    col_total = sky_cube.shape[2]
    channel_total = chan_count * freq_count
    block_cols = col_total // freq_count
    weights = free_mask.astype(jnp.bfloat16)
    masked_part = jnp.einsum("c,cyx->yx", weights, sky_cube, preferred_element_type=jnp.float32)
    count_part = jnp.sum(free_mask.astype(jnp.float32))
    masked_total, free_count = lax.psum((masked_part, count_part), "freq")
    baseline = masked_total / jnp.maximum(free_count, 1.0)
    flattened = (sky_cube.astype(jnp.float32) - baseline[None]).astype(jnp.bfloat16)[None, None]
    chan_start = freq_pos * chan_count
    rimmed = padded_2(flattened, (("freq", 2), ("sky", 3)), 1)
    first_layer = jax.nn.relu(conv_volume(rimmed, conv_first, [(0, 0), (0, 0), (1, 1)])).astype(
        jnp.bfloat16
    )
    feature_rimmed = padded_2(first_layer, (("freq", 2), ("sky", 3)), 1)
    second_layer = jax.nn.relu(conv_volume(feature_rimmed, conv_second, [(0, 0), (0, 0), (1, 1)]))
    local_channels = chan_start + jnp.arange(chan_count, dtype=jnp.int32)
    velocity = (local_channels.astype(jnp.float32) + 0.5) / channel_total - 0.5
    partial_value = project_moments(second_layer[0], velocity, channel_total)
    moment_whole = lax.psum(partial_value, "freq")
    moment_maps = moment_whole.astype(jnp.bfloat16)
    padded = jnp.pad(moment_maps, ((0, 0), (0, 0), (1, 1)))
    own_columns = lax.dynamic_slice_in_dim(padded, freq_pos * block_cols, block_cols + 2, 2)
    framed = padded_2(own_columns, (("sky", 1),), 1)
    return propose(
        framed, proposal_conv, score_head, box_head, sky_pos * row_count, freq_pos * block_cols
    )


def solution(mesh):
    in_specs = (P("freq", "sky", None), P("freq"), P(), P(), P(), P(), P())
    out_specs = (P(None, "sky", "freq"), P(None, None, "sky", "freq"))
    return jax.shard_map(
        on_device, mesh=mesh, in_specs=in_specs, out_specs=out_specs, check_vma=False
    )
```

profile of v0, /device:TPU:1, one launch (start us, length us, event | category | flops | bytes accessed | tf_op | source)
XLA Modules:
  0.0 438.8 jit_solution(8996807263624583406)
XLA Ops:
  0.7 1.3 convert_reduce_fusion
  2.0 0.9 fusion.28
  2.9 127.3 %all-reduce.1 = (f32[2,2048]{1,0:T(2,128)S(1)}, f32[]{:T(128)}) all-reduce(f32[2,2048]{1,0:T(2,128)S(1)} %bitcast.94, f32[]{:T(128)} %convert_reduce_fusion), channel_id=1, replica_groups=mesh['freq'=32,'sky'=16] {'freq'}, use_global_device_ids=true, to_apply=%region_0.0 | all-reduce | flops 4097 | bytes 32776 | tf_op jit(solution)/shard_map/psum | solution.py:94
  130.9 0.7 fusion.27
  131.6 1.3 collective-permute-start
  132.9 1.3 collective-permute-start.1
  134.2 4.6 %collective-permute-done.1 = bf16[1,1,1,2,2048]{4,3,2,1,0:T(2,128)(2,1)S(1)} collective-permute-done((bf16[1,1,1,2,2048]{4,3,2,1,0:T(2,128)(2,1)S(1)}, bf16[1,1,1,2,2048]{4,3,2,1,0:T(2,128)(2,1)S(1)}, u32[]{:S(2)}, u32[]{:S(2)}) %collective-permute-start.1) | collective-permute-done | bytes 8224 | tf_op jit(solution)/shard_map/ppermute | solution.py:15
  138.9 31.8 %collective-permute-start.2 = (bf16[1,1,4,1,2048]{4,3,2,1,0:T(2,128)(2,1)S(1)}, bf16[1,1,4,1,2048]{4,3,2,1,0:T(2,128)(2,1)S(1)}, u32[]{:S(2)}, u32[]{:S(2)}) collective-permute-start(bf16[1,1,4,1,2048]{4,3,2,1,0:T(2,128)(2,1)S(1)} %get-tuple-element.24), channel_id=1, source_target_pairs={{0,1},{1,2},{2,3},{3,4},{4,5},{5,6},{6,7},{7,8},{8,9},{9,10},{10,1... | collective-permute-start | bytes 49160 | tf_op jit(solution)/shard_map/ppermute | solution.py:12
  170.7 1.9 collective-permute-start.3
  172.6 3.3 collective-permute-done.3
  176.2 0.2 reshape.55
  176.5 4.0 copy.49
  180.5 9.4 %maximum_convert_fusion = bf16[2,2,8,257,32]{4,2,3,1,0:T(8,128)(2,1)S(1)} fusion(bf16[1,4,4,8,259]{3,0,4,2,1:T(2,128)(2,1)} %copy.49, pred[8,257]{0,1:T(8,128)(4,1)S(1)} %copy-done.5, bf16[32,1,3,3,3]{0,4,3,2,1:T(4,128)(2,1)S(1)} %copy-done.4), kind=kOutput, calls=%fused_computation.10 | convolution fusion | flops 15000576 | bytes 596424 | tf_op jit(solution)/shard_map/conv_general_dilated | solution.py:21
  189.9 1.1 fusion.66
  191.0 2.2 copy.52
  193.3 1.9 copy.51
  195.2 0.3 reshape.59
  195.5 6.1 %collective-permute-start.4 = (bf16[1,32,1,2,2048]{4,1,3,0,2:T(8,128)(2,1)S(1)}, bf16[1,32,1,2,2048]{4,1,3,0,2:T(8,128)(2,1)S(1)}, u32[]{:S(2)}, u32[]{:S(2)}) collective-permute-start(bf16[1,32,1,2,2048]{4,1,3,0,2:T(8,128)(2,1)S(1)} %slice_bitcast_fusion.3), channel_id=1, source_target_pairs={{0,16},{16,32},{32,48},{48,64},{64,80},{80,96},{96,112},{112,128},... | collective-permute-start | bytes 786440 | tf_op jit(solution)/shard_map/ppermute | solution.py:12
  201.6 0.8 copy.53
  202.4 0.3 reshape.61
  202.7 1.3 collective-permute-start.5
  204.0 0.6 reshape.77
  204.7 7.0 %collective-permute-done.4 = bf16[1,32,1,2,2048]{4,1,3,0,2:T(8,128)(2,1)S(1)} collective-permute-done((bf16[1,32,1,2,2048]{4,1,3,0,2:T(8,128)(2,1)S(1)}, bf16[1,32,1,2,2048]{4,1,3,0,2:T(8,128)(2,1)S(1)}, u32[]{:S(2)}, u32[]{:S(2)}) %collective-permute-start.4) | collective-permute-done | bytes 262176 | tf_op jit(solution)/shard_map/ppermute | solution.py:12
  211.6 1.1 collective-permute-done.5
  213.0 2.4 collective-permute-start.6
  215.4 1.9 collective-permute-start.7
  217.4 4.1 collective-permute-done.6
  221.5 10.0 %collective-permute-done.7 = bf16[1,32,4,1,2048]{4,1,3,2,0:T(8,128)(2,1)S(1)} collective-permute-done((bf16[1,32,4,1,2048]{4,1,3,2,0:T(8,128)(2,1)S(1)}, bf16[1,32,4,1,2048]{4,1,3,2,0:T(8,128)(2,1)S(1)}, u32[]{:S(2)}, u32[]{:S(2)}) %collective-permute-start.7) | collective-permute-done | bytes 524320 | tf_op jit(solution)/shard_map/ppermute | solution.py:15
  231.5 0.3 maximum_bitcast_fusion
  231.8 3.0 pad.7
  234.8 5.4 %reshape.64 = bf16[32,4,4,1,8,257]{5,4,0,2,1,3:T(8,128)(2,1)S(1)} reshape(bf16[32,4,4,1,2056]{4,0,2,1,3:T(8,128)(2,1)} %pad.7) | data formatting | bytes 4210688 | tf_op jit(solution)/shard_map/conv_general_dilated | solution.py:21
  240.2 7.8 %copy.57 = bf16[32,4,4,1,8,257]{0,4,5,2,1,3:T(8,128)(2,1)} copy(bf16[32,4,4,1,8,257]{5,4,0,2,1,3:T(8,128)(2,1)S(1)} %reshape.64) | data formatting | bytes 4210688 | tf_op jit(solution)/shard_map/conv_general_dilated | solution.py:21
  248.0 0.9 slice.78
  248.8 15.6 %select_maximum_fusion = f32[2,2,8,257,32]{4,2,3,1,0:T(8,128)} fusion(pred[8,257]{0,1:T(8,128)(4,1)S(1)} %copy-done.5, bf16[32,32,3,3,3]{1,0,4,3,2:T(8,128)(2,1)} %param.10, bf16[32,4,4,1,7,2]{0,4,5,2,1,3:T(8,128)(2,1)S(1)} %slice.78, bf16[32,4,4,1,8,257]{0,4,5,2,1,3:T(8,128)(2,1)} %copy.57), kind=kOutput, calls=%fused_computation.9 | convolution fusion | flops 461645824 | bytes 3229704 | tf_op jit(solution)/shard_map/conv_general_dilated | solution.py:21
  264.4 3.4 copy.58
  267.8 0.4 reshape.68
  268.4 4.0 fusion.13
  272.4 0.3 bitcast_multiply_fusion
  272.9 130.6 %all-reduce.3 = bf16[64,2,2048]{2,0,1:T(8,128)(2,1)S(1)} all-reduce(f32[64,2,2048]{2,0,1:T(8,128)S(1)} %pad_maximum_fusion.1), channel_id=1, replica_groups=mesh['freq'=32,'sky'=16] {'freq'}, use_global_device_ids=true, to_apply=%region_4.5 | all-reduce | flops 262144 | bytes 1572864 | tf_op jit(solution)/shard_map/psum | solution.py:107
  403.6 27.7 %collective-permute-start.8 = (bf16[64,1,66]{2,0,1:T(8,128)(2,1)S(1)}, bf16[64,1,66]{2,0,1:T(8,128)(2,1)S(1)}, u32[]{:S(2)}, u32[]{:S(2)}) collective-permute-start(bf16[64,1,66]{2,0,1:T(8,128)(2,1)S(1)} %get-tuple-element.16), channel_id=1, source_target_pairs={{0,1},{1,2},{2,3},{3,4},{4,5},{5,6},{6,7},{7,8},{8,9},{9,10},{10,1... | collective-permute-start | bytes 25352 | tf_op jit(solution)/shard_map/ppermute | solution.py:12
  431.3 1.9 collective-permute-start.9
  433.4 3.0 collective-permute-done.9
  436.4 0.1 copy.72
  436.7 0.3 fusion.12
  437.1 0.1 convolution_bitcast_fusion
  437.3 0.1 convolution_bitcast_fusion.1
  437.4 0.6 copy.65
  438.2 0.6 maximum_multiply_fusion
  (47 shorter events, 1.6 us)
Async XLA Ops:
  0.6 436.0 %copy-start = (bf16[3,3,64,256]{3,2,1,0:T(8,128)(2,1)S(1)}, bf16[3,3,64,256]{3,2,1,0:T(8,128)(2,1)}, u32[]{:S(2)}) copy-start(bf16[3,3,64,256]{3,2,1,0:T(8,128)(2,1)} %param.11) | copy-start | bytes 884740
  0.6 179.8 %copy-start.5 = (pred[8,257]{0,1:T(8,128)(4,1)S(1)}, pred[8,257]{0,1:T(8,128)(4,1)}, u32[]{:S(2)}) copy-start(pred[8,257]{0,1:T(8,128)(4,1)} %constant.85) | copy-start | bytes 6172
  0.7 179.8 %copy-start.4 = (bf16[32,1,3,3,3]{0,4,3,2,1:T(4,128)(2,1)S(1)}, bf16[32,1,3,3,3]{0,4,3,2,1:T(4,128)(2,1)}, u32[]{:S(2)}) copy-start(bf16[32,1,3,3,3]{0,4,3,2,1:T(4,128)(2,1)} %param.9) | copy-start | bytes 5188
  131.6 2.6 collective-permute-start
  132.9 5.9 %collective-permute-start.1 = (bf16[1,1,1,2,2048]{4,3,2,1,0:T(2,128)(2,1)S(1)}, bf16[1,1,1,2,2048]{4,3,2,1,0:T(2,128)(2,1)S(1)}, u32[]{:S(2)}, u32[]{:S(2)}) collective-permute-start(bf16[1,1,1,2,2048]{4,3,2,1,0:T(2,128)(2,1)S(1)} %get-tuple-element.27), channel_id=1, source_target_pairs={{16,0},{32,16},{48,32},{64,48},{80,64},{96,80},{112,96},{128,112},... | collective-permute-start | bytes 24584 | tf_op jit(solution)/shard_map/ppermute | solution.py:15
  138.9 33.7 %collective-permute-start.2 = (bf16[1,1,4,1,2048]{4,3,2,1,0:T(2,128)(2,1)S(1)}, bf16[1,1,4,1,2048]{4,3,2,1,0:T(2,128)(2,1)S(1)}, u32[]{:S(2)}, u32[]{:S(2)}) collective-permute-start(bf16[1,1,4,1,2048]{4,3,2,1,0:T(2,128)(2,1)S(1)} %get-tuple-element.24), channel_id=1, source_target_pairs={{0,1},{1,2},{2,3},{3,4},{4,5},{5,6},{6,7},{7,8},{8,9},{9,10},{10,1... | collective-permute-start | bytes 49160 | tf_op jit(solution)/shard_map/ppermute | solution.py:12
  170.7 5.2 %collective-permute-start.3 = (bf16[1,1,4,1,2048]{4,3,2,1,0:T(2,128)(2,1)S(1)}, bf16[1,1,4,1,2048]{4,3,2,1,0:T(2,128)(2,1)S(1)}, u32[]{:S(2)}, u32[]{:S(2)}) collective-permute-start(bf16[1,1,4,1,2048]{4,3,2,1,0:T(2,128)(2,1)S(1)} %get-tuple-element.25), channel_id=1, source_target_pairs={{1,0},{2,1},{3,2},{4,3},{5,4},{6,5},{7,6},{8,7},{9,8},{10,9},{11,1... | collective-permute-start | bytes 49160 | tf_op jit(solution)/shard_map/ppermute | solution.py:15
  195.2 8.8 %copy-start.1 = (bf16[2,2,8,257,32]{3,2,4,1,0:T(8,128)(2,1)S(1)}, bf16[2,2,8,257,32]{3,2,4,1,0:T(8,128)(2,1)}, u32[]{:S(2)}) copy-start(bf16[2,2,8,257,32]{3,2,4,1,0:T(8,128)(2,1)} %copy.52) | copy-start | bytes 1579012
  195.5 16.1 %collective-permute-start.4 = (bf16[1,32,1,2,2048]{4,1,3,0,2:T(8,128)(2,1)S(1)}, bf16[1,32,1,2,2048]{4,1,3,0,2:T(8,128)(2,1)S(1)}, u32[]{:S(2)}, u32[]{:S(2)}) collective-permute-start(bf16[1,32,1,2,2048]{4,1,3,0,2:T(8,128)(2,1)S(1)} %slice_bitcast_fusion.3), channel_id=1, source_target_pairs={{0,16},{16,32},{32,48},{48,64},{64,80},{80,96},{96,112},{112,128},... | collective-permute-start | bytes 786440 | tf_op jit(solution)/shard_map/ppermute | solution.py:12
  202.7 10.0 %collective-permute-start.5 = (bf16[1,32,1,2,2048]{4,1,3,2,0:T(8,128)(2,1)S(1)}, bf16[1,32,1,2,2048]{4,1,3,2,0:T(8,128)(2,1)S(1)}, u32[]{:S(2)}, u32[]{:S(2)}) collective-permute-start(bf16[1,32,1,2,2048]{4,1,3,2,0:T(8,128)(2,1)S(1)} %slice_bitcast_fusion.2), channel_id=1, source_target_pairs={{16,0},{32,16},{48,32},{64,48},{80,64},{96,80},{112,96},{128,112},... | collective-permute-start | bytes 786440 | tf_op jit(solution)/shard_map/ppermute | solution.py:15
  213.0 8.5 %collective-permute-start.6 = (bf16[1,32,4,1,2048]{4,1,3,2,0:T(8,128)(2,1)S(1)}, bf16[1,32,4,1,2048]{4,1,3,2,0:T(8,128)(2,1)S(1)}, u32[]{:S(2)}, u32[]{:S(2)}) collective-permute-start(bf16[1,32,4,1,2048]{4,1,3,2,0:T(8,128)(2,1)S(1)} %get-tuple-element.14), channel_id=1, source_target_pairs={{0,1},{1,2},{2,3},{3,4},{4,5},{5,6},{6,7},{7,8},{8,9},{9,10},{10,1... | collective-permute-start | bytes 1572872 | tf_op jit(solution)/shard_map/ppermute | solution.py:12
  215.4 16.1 %collective-permute-start.7 = (bf16[1,32,4,1,2048]{4,1,3,2,0:T(8,128)(2,1)S(1)}, bf16[1,32,4,1,2048]{4,1,3,2,0:T(8,128)(2,1)S(1)}, u32[]{:S(2)}, u32[]{:S(2)}) collective-permute-start(bf16[1,32,4,1,2048]{4,1,3,2,0:T(8,128)(2,1)S(1)} %get-tuple-element.15), channel_id=1, source_target_pairs={{1,0},{2,1},{3,2},{4,3},{5,4},{6,5},{7,6},{8,7},{9,8},{10,9},{11,1... | collective-permute-start | bytes 1572872 | tf_op jit(solution)/shard_map/ppermute | solution.py:15
  272.9 163.8 %copy-start.6 = (pred[8,9]{0,1:T(8,128)(4,1)S(1)}, pred[8,9]{0,1:T(8,128)(4,1)}, u32[]{:S(2)}) copy-start(pred[8,9]{0,1:T(8,128)(4,1)} %constant.84) | copy-start | bytes 220
  272.9 164.2 %copy-start.2 = (bf16[36,256]{1,0:T(8,128)(2,1)S(1)}, bf16[36,256]{1,0:T(8,128)(2,1)}, u32[]{:S(2)}) copy-start(bf16[36,256]{1,0:T(8,128)(2,1)} %param.13) | copy-start | bytes 55300
  272.9 164.4 %copy-start.3 = (bf16[9,256]{1,0:T(8,128)(2,1)S(1)}, bf16[9,256]{1,0:T(8,128)(2,1)}, u32[]{:S(2)}) copy-start(bf16[9,256]{1,0:T(8,128)(2,1)} %param.12) | copy-start | bytes 13828
  403.6 29.7 %collective-permute-start.8 = (bf16[64,1,66]{2,0,1:T(8,128)(2,1)S(1)}, bf16[64,1,66]{2,0,1:T(8,128)(2,1)S(1)}, u32[]{:S(2)}, u32[]{:S(2)}) collective-permute-start(bf16[64,1,66]{2,0,1:T(8,128)(2,1)S(1)} %get-tuple-element.16), channel_id=1, source_target_pairs={{0,1},{1,2},{2,3},{3,4},{4,5},{5,6},{6,7},{7,8},{8,9},{9,10},{10,1... | collective-permute-start | bytes 25352 | tf_op jit(solution)/shard_map/ppermute | solution.py:12
  431.3 5.1 %collective-permute-start.9 = (bf16[64,1,66]{2,0,1:T(8,128)(2,1)S(1)}, bf16[64,1,66]{2,0,1:T(8,128)(2,1)S(1)}, u32[]{:S(2)}, u32[]{:S(2)}) collective-permute-start(bf16[64,1,66]{2,0,1:T(8,128)(2,1)S(1)} %get-tuple-element.17), channel_id=1, source_target_pairs={{1,0},{2,1},{3,2},{4,3},{5,4},{6,5},{7,6},{8,7},{9,8},{10,9},{11,1... | collective-permute-start | bytes 25352 | tf_op jit(solution)/shard_map/ppermute | solution.py:15
where the time goes:
time: 442 us; the launch traced here: 439 us
  blocking collectives  258 us (58%)
  starting transfers between devices  77.6 us (18%)
  local copies, waits for them, and re-layouts  34 us (8%)
  waiting for transfers between devices  33.1 us (7%)
  matrix products  30.4 us (7%)
    psum x1, blocking collectives, on_device(): moment_whole = lax.psum(partial_value, 'freq')  131 us
    psum x1, blocking collectives, on_device(): masked_total, free_count = lax.psum((masked_part, count_part), 'freq')  127 us
    ppermute x5, starting transfers between devices, padded_2(): lax.ppermute(lax.slice_in_dim(block, block.shape[dim] - width, None, axis...  69.2 us
    conv_general_dilated x2, matrix products, conv_volume(): lax.conv_general_dilated(volume, kernel, (1, 1, 1), paddings, dimension_n...  25 us
    ppermute x5, waiting for transfers between devices, padded_2(): lax.ppermute(lax.slice_in_dim(block, 0, width, axis=dim), axis, backward)  22 us
    conv_general_dilated x6, local copies, waits for them, and re-layouts, conv_volume(): lax.conv_general_dilated(volume, kernel, (1, 1, 1), paddings, dimension_n...  18.3 us
    ppermute x5, waiting for transfers between devices, padded_2(): lax.ppermute(lax.slice_in_dim(block, block.shape[dim] - width, None, axis...  11.1 us
  transfers between devices with their start and end apart: 10, of which 7 were waited for; matrix products, arithmetic and copies ran while one was open for 0% of the time, Pallas kernels for 0%

commit v1 on v0

v1 whole, which is shorter than its diff:
```python
import functools

import jax
import jax.numpy as jnp
from jax import lax
from jax.experimental import pallas as pl
from jax.experimental.pallas import tpu as pltpu
from jax.sharding import PartitionSpec as P

F32 = jnp.float32
BF16 = jnp.bfloat16
MESH = pl.DeviceIdType.MESH
CHANS = 64
FEAT = 32
ANCHORS = 9
WIDTH = 64
LANES = 128
SLAB = 16
STRIDE = 5
ROWS_ONE = (STRIDE + 2) * SLAB
ROWS_TWO = STRIDE * SLAB
PAIRS = CHANS // 2 + 1
STEP = 2 * 6 * FEAT
SPAN = 2 * STEP
WINDOW = 8
WINDOW_LANES = WINDOW * 6 * FEAT
GROUP = 3
NT = (((1,), (1,)), ((), ()))


def iota(shape, dim):
    return lax.broadcasted_iota(jnp.int32, shape, dim)


def dot(a, b):
    return jnp.dot(a, b, preferred_element_type=F32)


def dot_nt(a, b):
    return lax.dot_general(a, b, NT, preferred_element_type=F32)


def fill_tx(cube, free, tx):
    chans, rows, cols = cube.shape
    lines = chans * rows
    values = cube[...].astype(F32).reshape(lines, cols)
    line = iota((lines, LANES), 0)
    lane = iota((lines, LANES), 1)
    marks = jnp.zeros((lines, LANES), F32)
    flags = free[...].astype(F32)
    for c in range(chans):
        marks = jnp.where(line // rows == c, flags[0:1, c : c + 1], marks)
    even = jnp.concatenate([values[:, cols - 3 :], values[:, : cols - 3]], axis=1)
    odd = jnp.concatenate([values[:, WIDTH - 3 :], values[:, : WIDTH - 3]], axis=1)
    for block in range(cols // WIDTH):
        source = odd if block % 2 else even
        start = block // 2 * LANES
        piece = source[:, start : start + LANES]
        tx[block] = jnp.where(lane == LANES - 1, marks, piece).astype(BF16)


def fill_first(taps, sky, height, w_one):
    spread = (iota((FEAT, LANES), 1) % FEAT == iota((FEAT, LANES), 0)).astype(BF16)
    rows = dot(taps, spread)
    r = iota((8, LANES), 0)
    lane = iota((8, LANES), 1)
    zero = jnp.zeros((8, LANES), F32)
    for tile in range(WINDOW_LANES // LANES):
        block = 4 * tile + lane // FEAT
        q = block % 6
        b = block // 6
        y = 2 * sky - 2 + q
        inside = (y >= 0) & (y < height)
        row_masks = [(r - q == dy) & inside for dy in range(3)]
        b_values = sorted({(4 * tile) // 6, (4 * tile + 3) // 6})
        masks = {}
        for bv in b_values:
            for dy in range(3):
                masks[bv, dy] = row_masks[dy] & (b == bv) if len(b_values) > 1 else row_masks[dy]
        for dx in range(3):
            parts = []
            for a in range(10):
                value = zero
                for bv in b_values:
                    dc = a - bv
                    if 0 <= dc <= 2:
                        for dy in range(3):
                            tap = (dc * 3 + dy) * 3 + dx
                            value = jnp.where(masks[bv, dy], rows[tap : tap + 1, :], value)
                parts.append(value)
            for half in range(5):
                both = jnp.concatenate([parts[2 * half], parts[2 * half + 1]], axis=0)
                base = 80 * dx + 16 * half
                w_one[base : base + 16, tile * LANES : (tile + 1) * LANES] = both.astype(BF16)
        w_one[240:256, tile * LANES : (tile + 1) * LANES] = jnp.zeros((16, LANES), BF16)


def fill_second(kernel, spread_taps, w_two):
    eye = (iota((FEAT, FEAT), 0) == iota((FEAT, FEAT), 1)).astype(BF16)
    source = iota((LANES, 4 * LANES), 0)
    target = iota((LANES, 4 * LANES), 1)
    spread = (source == target // LANES * FEAT + target % FEAT).astype(BF16)
    for t in range(7):
        count = min(4, 27 - 4 * t)
        part = kernel[4 * t : 4 * t + count].reshape(count * FEAT, FEAT)
        if count < 4:
            part = jnp.concatenate([part, jnp.zeros(((4 - count) * FEAT, FEAT), BF16)], axis=0)
        turned = dot_nt(eye, part).astype(BF16)
        wide = dot(turned, spread).astype(BF16)
        for g in range(count):
            spread_taps[4 * t + g] = wide[:, g * LANES : (g + 1) * LANES]
    group = iota((FEAT, LANES), 1) // FEAT
    zero = jnp.zeros((FEAT, LANES), BF16)
    for dx in range(3):
        for cin in range(4):
            for yin in range(6):
                base = (cin * 6 + yin) * FEAT
                for cout in range(2):
                    value = zero
                    dc = cin - cout
                    if 0 <= dc <= 2:
                        for yout in range(4):
                            dy = yin - yout
                            if 0 <= dy <= 2:
                                tap = spread_taps[(dc * 3 + dy) * 3 + dx]
                                value = jnp.where(group == yout, tap, value)
                    w_two[dx, base : base + FEAT, cout * LANES : (cout + 1) * LANES] = value


def fill_proposal(kernel, w_prop):
    wide = kernel.shape[3]
    zero = jnp.zeros((FEAT, wide), BF16)
    for dx in range(3):
        for moment in range(2):
            for y in range(4):
                base = ((dx * 2 + moment) * 4 + y) * FEAT
                for yout in range(2):
                    dy = y - yout
                    value = zero
                    if 0 <= dy <= 2:
                        value = kernel[dy, dx, moment * FEAT : (moment + 1) * FEAT, :]
                    w_prop[base : base + FEAT, yout * wide : (yout + 1) * wide] = value


def fill_heads(score, box, heads):
    lines = heads.shape[0]

    def picked(count, wanted):
        row = iota((lines, count), 0)
        return (wanted(row // SLAB, row % SLAB) == iota((lines, count), 1)).astype(BF16)

    from_score = picked(ANCHORS, lambda g, k: jnp.where((g == 0) & (k < ANCHORS), k, -1))
    from_box = picked(4 * ANCHORS, lambda g, k: jnp.where((g > 0) & (k < ANCHORS), 4 * k + g - 1, -1))
    heads[...] = (dot(from_score, score[...]) + dot(from_box, box[...])).astype(BF16)


def flatten(rx, lines, planes, freq, cols):
    blocks, rows, _ = rx.shape
    values = rx[...].astype(F32)
    marks = values[:, :, LANES - 1 :]
    total = jnp.sum(values * marks, axis=0)
    count = jnp.sum(jnp.broadcast_to(marks, values.shape), axis=0)
    total = functools.reduce(jnp.add, [total[2 * c : 2 * c + 2] for c in range(rows // 2)])
    count = functools.reduce(jnp.add, [count[2 * c : 2 * c + 2] for c in range(rows // 2)])
    baseline = total / jnp.maximum(count, 1.0)
    baseline = jnp.concatenate([baseline] * (rows // 2), axis=0)
    col = WIDTH * freq - 3 + iota((rows, LANES), 1)
    inside = (col >= 0) & (col < cols)
    for block in range(blocks):
        lines[block * rows : (block + 1) * rows, :] = jnp.where(inside, values[block] - baseline, 0.0)
    for y in range(2):
        planes[3 + y] = lines[pl.ds(y, CHANS, stride=2), :].astype(BF16)


def fill_shifted(planes, lines, shifted, sky, height):
    for r in range(8):
        y = 2 * sky - 3 + r
        value = planes[r].astype(F32)
        if r not in (3, 4):
            value = jnp.where((y >= 0) & (y < height), value, 0.0)
        lines[CHANS * r : CHANS * (r + 1), :] = value
    zero = jnp.zeros((8, LANES), F32)
    for pair in range(PAIRS):
        both = []
        for c in (2 * pair - 1, 2 * pair):
            both.append(lines[pl.ds(c, 8, stride=CHANS), :] if 0 <= c < CHANS else zero)
        for dx in range(3):
            moved = both if dx == 0 else [pltpu.roll(v, LANES - dx, 1) for v in both]
            shifted[dx, 16 * pair : 16 * pair + 16, :] = jnp.concatenate(moved, axis=0).astype(BF16)


def convolve_first(shifted, w_one, layer, freq, cols):
    j = iota((ROWS_ONE, LANES), 0)
    x = j % SLAB * STRIDE + j // SLAB
    col = WIDTH * freq - 2 + x
    inside = (x < WIDTH + 4) & (col >= 0) & (col < cols)
    turn = ((iota((ROWS_ONE, LANES), 1) == x) & inside).astype(BF16)
    zero = jnp.zeros((16, LANES), BF16)
    edge = jnp.zeros((ROWS_ONE, STEP), BF16)
    layer[:, :STEP] = edge
    layer[:, STEP * PAIRS :] = edge
    for w in range(CHANS // WINDOW):
        parts = [shifted[dx, 64 * w : 64 * w + 80, :] for dx in range(3)]
        lhs = dot_nt(turn, jnp.concatenate(parts + [zero], axis=0)).astype(BF16)
        for n in range(WINDOW_LANES // 256):
            value = dot(lhs, w_one[:, 256 * n : 256 * n + 256])
            base = STEP + w * WINDOW_LANES + 256 * n
            layer[:, base : base + 256] = jnp.maximum(value, 0.0).astype(BF16)


def convolve_second(layer, w_two):
    zeroth = jnp.zeros((ROWS_TWO, LANES), F32)
    first = jnp.zeros((ROWS_TWO, LANES), F32)
    for start in range(0, PAIRS, GROUP):
        pairs = range(start, min(PAIRS, start + GROUP))
        total = None
        for dx in range(3):
            parts = [
                layer[SLAB * dx : SLAB * dx + ROWS_TWO, STEP * p : STEP * p + SPAN] for p in pairs
            ]
            part = dot(jnp.concatenate(parts, axis=0), w_two[dx])
            total = part if total is None else total + part
        total = jnp.maximum(total, 0.0)
        for i, p in enumerate(pairs):
            for half in range(2):
                c = 2 * p - 1 + half
                if 0 <= c < CHANS:
                    value = total[
                        ROWS_TWO * i : ROWS_TWO * (i + 1), LANES * half : LANES * (half + 1)
                    ]
                    zeroth = zeroth + value
                    first = first + ((c + 0.5) / CHANS - 0.5) * value
    return zeroth * (1.0 / CHANS), first * (12.0 / CHANS)


def propose(zeroth, first, w_prop, heads, freq, sky, height, cols, objectness, proposals):
    maps = jnp.concatenate([zeroth, first], axis=1)
    y = 2 * sky - 1 + iota(maps.shape, 1) // FEAT % 4
    maps = jnp.where((y >= 0) & (y < height), maps, 0.0).astype(BF16)
    row = iota((3 * WIDTH, ROWS_TWO), 0)
    x = row % WIDTH + row // WIDTH
    col = WIDTH * freq - 1 + x
    j = iota((3 * WIDTH, ROWS_TWO), 1)
    turn = ((j % SLAB * STRIDE + j // SLAB == x) & (col >= 0) & (col < cols)).astype(BF16)
    framed = dot(turn, maps).astype(BF16)
    framed = jnp.concatenate([framed[WIDTH * dx : WIDTH * (dx + 1)] for dx in range(3)], axis=1)
    hidden = jnp.maximum(dot(framed, w_prop[...]), 0.0).astype(BF16)
    k = iota((SLAB, WIDTH), 0)
    anchor_width = jnp.ones((SLAB, WIDTH), F32)
    anchor_height = anchor_width
    for anchor in range(ANCHORS):
        scale = 4.0 * 2.0 ** (anchor // 3)
        root = (2.0 ** (anchor % 3 - 1)) ** 0.5
        anchor_width = jnp.where(k == anchor, scale * root, anchor_width)
        anchor_height = jnp.where(k == anchor, scale / root, anchor_height)
    centre_col = (WIDTH * freq + iota((SLAB, WIDTH), 1)).astype(F32) + 0.5
    wide = hidden.shape[1] // 2
    for row in range(2):
        out = dot_nt(heads[...], hidden[:, wide * row : wide * (row + 1)])
        score, dx, dy, dw, dh = [out[SLAB * g : SLAB * (g + 1)] for g in range(5)]
        centre_row = (2 * sky + row).astype(F32) + 0.5
        centre_x = centre_col + dx * anchor_width
        centre_y = centre_row + dy * anchor_height
        half_width = 0.5 * (anchor_width * jnp.exp(dw))
        half_height = 0.5 * (anchor_height * jnp.exp(dh))
        objectness[:, row, :] = score[:ANCHORS]
        corners = (
            centre_x - half_width,
            centre_y - half_height,
            centre_x + half_width,
            centre_y + half_height,
        )
        for side, corner in enumerate(corners):
            proposals[:, side, row, :] = (corner * (1.0 / 64.0))[:ANCHORS]


def body(
    shape,
    cube_hbm, free_hbm, taps_hbm, kernel_hbm, proposal_hbm, score_hbm, box_hbm,
    objectness, proposals,
    cube, free, taps, kernel, proposal, score, box,
    tx, rx, planes, lines, lines_all, shifted, w_one, spread_taps, w_two, w_prop, heads, layer,
    load_sem, send_sem, recv_sem, halo_send, halo_recv,
):
    freq_count, sky_count, height, cols = shape
    freq = lax.axis_index("freq")
    sky = lax.axis_index("sky")
    barrier = pltpu.get_barrier_semaphore()

    def freq_peer(i):
        return {"freq": lax.rem(freq + i, freq_count)}

    def sky_peer(i):
        return {"sky": lax.rem(sky + i + sky_count, sky_count)}

    def greet(i, carry):
        pl.semaphore_signal(barrier, inc=1, device_id=freq_peer(i), device_id_type=MESH)
        return carry

    lax.fori_loop(1, freq_count, greet, 0)
    for i in (-2, -1, 1, 2):
        pl.semaphore_signal(barrier, inc=1, device_id=sky_peer(i), device_id_type=MESH)

    moves = (
        (cube_hbm, cube), (free_hbm, free), (taps_hbm, taps), (kernel_hbm, kernel),
        (proposal_hbm, proposal), (score_hbm, score), (box_hbm, box),
    )
    loads = [
        pltpu.make_async_copy(source, target, load_sem.at[i])
        for i, (source, target) in enumerate(moves)
    ]
    for load in loads:
        load.start()
    loads[0].wait()
    loads[1].wait()
    fill_tx(cube, free, tx)

    def exchange(i):
        return pltpu.make_async_remote_copy(
            src_ref=tx.at[lax.rem(freq + i, freq_count)],
            dst_ref=rx.at[freq],
            send_sem=send_sem.at[i],
            recv_sem=recv_sem.at[i],
            device_id=freq_peer(i),
            device_id_type=MESH,
        )

    def send(i, carry):
        exchange(i).start()
        return carry

    def finish(i, carry):
        exchange(i).wait()
        return carry

    pl.semaphore_wait(barrier, freq_count + 3)
    lax.fori_loop(1, freq_count, send, 0)
    rx[freq] = tx[freq]
    for load in loads[2:]:
        load.wait()
    fill_first(taps[...], sky, height, w_one)
    fill_second(kernel, spread_taps, w_two)
    fill_proposal(proposal, w_prop)
    fill_heads(score, box, heads)
    lax.fori_loop(1, freq_count, finish, 0)

    flatten(rx, lines, planes, freq, cols)
    halos = []
    for n, (i, source, target) in enumerate(((1, 3, 1), (-1, 3, 5), (2, 4, 0), (-2, 3, 7))):
        size = 2 if abs(i) == 1 else 1
        halos.append(
            pltpu.make_async_remote_copy(
                src_ref=planes.at[pl.ds(source, size)],
                dst_ref=planes.at[pl.ds(target, size)],
                send_sem=halo_send.at[n],
                recv_sem=halo_recv.at[n],
                device_id=sky_peer(i),
                device_id_type=MESH,
            )
        )
    for halo in halos:
        halo.start()
    for halo in halos:
        halo.wait()
    fill_shifted(planes, lines_all, shifted, sky, height)
    convolve_first(shifted, w_one, layer, freq, cols)
    zeroth, first = convolve_second(layer, w_two)
    propose(zeroth, first, w_prop, heads, freq, sky, height, cols, objectness, proposals)


def on_device(sky_cube, free_mask, conv_first, conv_second, proposal_conv, score_head, box_head):
    freq_count = lax.axis_size("freq")
    sky_count = lax.axis_size("sky")
    chans, rows, cols = sky_cube.shape
    wide = proposal_conv.shape[3]
    taps = conv_first.transpose(1, 2, 3, 4, 0).reshape(27, FEAT)
    kernel = conv_second.transpose(2, 3, 4, 0, 1).reshape(27, FEAT, FEAT)
    free = free_mask.reshape(1, chans)
    operands = (sky_cube, free, taps, kernel, proposal_conv, score_head, box_head)
    scratch = [pltpu.VMEM(operand.shape, operand.dtype) for operand in operands] + [
        pltpu.VMEM((freq_count, chans * rows, LANES), BF16),
        pltpu.VMEM((freq_count, chans * rows, LANES), BF16),
        pltpu.VMEM((8, CHANS, LANES), BF16),
        pltpu.VMEM((2 * CHANS, LANES), F32),
        pltpu.VMEM((8 * CHANS, LANES), F32),
        pltpu.VMEM((3, 16 * PAIRS, LANES), BF16),
        pltpu.VMEM((256, WINDOW_LANES), BF16),
        pltpu.VMEM((27, FEAT, LANES), BF16),
        pltpu.VMEM((3, SPAN, 256), BF16),
        pltpu.VMEM((3 * 256, 2 * wide), BF16),
        pltpu.VMEM((5 * SLAB, wide), BF16),
        pltpu.VMEM((ROWS_ONE, STEP * (PAIRS + 1)), BF16),
        pltpu.SemaphoreType.DMA((len(operands),)),
        pltpu.SemaphoreType.DMA((freq_count,)),
        pltpu.SemaphoreType.DMA((freq_count,)),
        pltpu.SemaphoreType.DMA((4,)),
        pltpu.SemaphoreType.DMA((4,)),
    ]
    shape = (freq_count, sky_count, rows * sky_count, cols)
    return pl.pallas_call(
        functools.partial(body, shape),
        out_shape=(
            jax.ShapeDtypeStruct((ANCHORS, rows, WIDTH), F32),
            jax.ShapeDtypeStruct((ANCHORS, 4, rows, WIDTH), F32),
        ),
        in_specs=[pl.BlockSpec(memory_space=pl.ANY)] * len(operands),
        out_specs=(pl.BlockSpec(memory_space=pltpu.VMEM),) * 2,
        scratch_shapes=scratch,
        compiler_params=pltpu.CompilerParams(
            collective_id=0, has_side_effects=True, vmem_limit_bytes=40 * 1024 * 1024
        ),
    )(*operands)


def solution(mesh):
    in_specs = (P("freq", "sky", None), P("freq"), P(), P(), P(), P(), P())
    out_specs = (P(None, "sky", "freq"), P(None, None, "sky", "freq"))
    return jax.shard_map(
        on_device, mesh=mesh, in_specs=in_specs, out_specs=out_specs, check_vma=False
    )
```

time: 442 us -> 42 us (0.10)
  the two profiles are of different devices: /device:TPU:1 before, /device:TPU:4 now
where the time goes in v1:
time: 42 us; the launch traced here: 41.7 us
  Pallas kernels  35.7 us (85%)
  local copies, waits for them, and re-layouts  5.26 us (13%)
  between operations  0.68 us (2%)
    pallas_call x1, Pallas kernels, on_device(): pl.pallas_call(functools.partial(body, shape), out_shape=(jax.ShapeDtypeS...  35.7 us
    unnamed x14, local copies, waits for them, and re-layouts  4.53 us

profile of v1, /device:TPU:4, one launch (start us, length us, event | category | flops | bytes accessed | tf_op | source)
XLA Modules:
  0.0 41.7 jit_solution(14064670096922428720)
XLA Ops:
  0.6 0.0 copy-start.2
  0.6 0.0 copy-start.5
  0.7 0.7 %reshape.14.taps_hbm = bf16[27,32]{1,0:T(8,128)(2,1)S(1)} reshape(bf16[1,3,3,3,32]{4,3,2,1,0:T(4,128)(2,1)} %bitcast.7) | data formatting | bytes 3456 | tf_op jit(solution)/shard_map/reshape | solution.py:376
  1.4 0.0 copy-done.2
  1.4 0.0 copy-done.5
  1.4 0.0 copy-start
  1.4 1.0 %copy-done = bf16[3,3,64,256]{3,2,1,0:T(8,128)(2,1)S(1)} copy-done((bf16[3,3,64,256]{3,2,1,0:T(8,128)(2,1)S(1)}, bf16[3,3,64,256]{3,2,1,0:T(8,128)(2,1)}, u32[]{:S(2)}) %copy-start) | copy-done | bytes 294936
  2.4 0.0 copy-start.1
  2.4 0.9 %copy-done.1 = bf16[32,32,3,3,3]{1,0,4,3,2:T(8,128)(2,1)S(1)} copy-done((bf16[32,32,3,3,3]{1,0,4,3,2:T(8,128)(2,1)S(1)}, bf16[32,32,3,3,3]{1,0,4,3,2:T(8,128)(2,1)}, u32[]{:S(2)}) %copy-start.1) | copy-done | bytes 55320
  3.3 0.0 copy-start.3
  3.3 0.7 %copy-done.3 = bf16[2,2,2048]{2,1,0:T(2,128)(2,1)S(1)} copy-done((bf16[2,2,2048]{2,1,0:T(2,128)(2,1)S(1)}, bf16[2,2,2048]{2,1,0:T(2,128)(2,1)}, u32[]{:S(2)}) %copy-start.3) | copy-done | bytes 16408
  4.0 0.0 copy-start.4
  4.0 0.7 %copy-done.4 = bf16[9,256]{1,0:T(8,128)(2,1)S(1)} copy-done((bf16[9,256]{1,0:T(8,128)(2,1)S(1)}, bf16[9,256]{1,0:T(8,128)(2,1)}, u32[]{:S(2)}) %copy-start.4) | copy-done | bytes 4632
  4.7 35.7 %shard_map.86 = (f32[9,2,64]{2,1,0:T(2,128)S(1)}, f32[9,4,2,64]{3,2,1,0:T(2,128)S(1)}) custom-call(bf16[2,2,2048]{2,1,0:T(2,128)(2,1)S(1)} %copy-done.3, s32[1,2]{1,0:T(1,128)S(1)} %bitcast.6, bf16[27,32]{1,0:T(8,128)(2,1)S(1)} %reshape.14.taps_hbm, bf16[27,32,32]{2,1,0:T(8,128)(2,1)S(1)} %bitcast.5, bf16[3,3,64,256]{3,2,1,0:T(8,128)(2,1)S(1)} %copy-done, ...), custom_call_target="tpu_custom_call" | custom-call | tf_op jit(solution)/shard_map/pallas_call | solution.py:400
  40.5 0.6 %copy.11 = f32[9,2,64]{2,1,0:T(2,128)} copy(f32[9,2,64]{2,1,0:T(2,128)S(1)} %get-tuple-element.4) | data formatting | bytes 9216
  41.1 0.6 %copy.12 = f32[9,4,2,64]{3,2,1,0:T(2,128)} copy(f32[9,4,2,64]{3,2,1,0:T(2,128)S(1)} %get-tuple-element.5) | data formatting | bytes 36864
Async XLA Ops:
  0.6 0.8 %copy-start.2 = (bf16[36,256]{1,0:T(8,128)(2,1)S(1)}, bf16[36,256]{1,0:T(8,128)(2,1)}, u32[]{:S(2)}) copy-start(bf16[36,256]{1,0:T(8,128)(2,1)} %box_hbm.1) | copy-start | bytes 55300
  0.6 0.7 %copy-start.5 = (s32[2]{0:T(128)S(1)}, s32[2]{0:T(128)}, u32[]{:S(2)}) copy-start(s32[2]{0:T(128)} %param.8) | copy-start | bytes 28
  1.4 1.0 %copy-start = (bf16[3,3,64,256]{3,2,1,0:T(8,128)(2,1)S(1)}, bf16[3,3,64,256]{3,2,1,0:T(8,128)(2,1)}, u32[]{:S(2)}) copy-start(bf16[3,3,64,256]{3,2,1,0:T(8,128)(2,1)} %proposal_hbm.1) | copy-start | bytes 884740
  2.4 0.9 %copy-start.1 = (bf16[32,32,3,3,3]{1,0,4,3,2:T(8,128)(2,1)S(1)}, bf16[32,32,3,3,3]{1,0,4,3,2:T(8,128)(2,1)}, u32[]{:S(2)}) copy-start(bf16[32,32,3,3,3]{1,0,4,3,2:T(8,128)(2,1)} %param.10) | copy-start | bytes 165892
  3.3 0.7 %copy-start.3 = (bf16[2,2,2048]{2,1,0:T(2,128)(2,1)S(1)}, bf16[2,2,2048]{2,1,0:T(2,128)(2,1)}, u32[]{:S(2)}) copy-start(bf16[2,2,2048]{2,1,0:T(2,128)(2,1)} %cube_hbm.1) | copy-start | bytes 49156
  4.0 0.7 %copy-start.4 = (bf16[9,256]{1,0:T(8,128)(2,1)S(1)}, bf16[9,256]{1,0:T(8,128)(2,1)}, u32[]{:S(2)}) copy-start(bf16[9,256]{1,0:T(8,128)(2,1)} %score_hbm.1) | copy-start | bytes 13828

commit v2 on v1

--- a/solution.py
+++ b/solution.py
@@ -16,15 +16,17 @@
 WIDTH = 64
 LANES = 128
 SLAB = 16
-STRIDE = 5
+HEAD = 16
+STRIDE = 9
 ROWS_ONE = (STRIDE + 2) * SLAB
 ROWS_TWO = STRIDE * SLAB
-PAIRS = CHANS // 2 + 1
+PAIRS = CHANS // 4
 STEP = 2 * 6 * FEAT
 SPAN = 2 * STEP
 WINDOW = 8
 WINDOW_LANES = WINDOW * 6 * FEAT
-GROUP = 3
+WINDOWS = CHANS // 2 // WINDOW
+GROUP = 4
 NT = (((1,), (1,)), ((), ()))
 
 
@@ -61,7 +63,7 @@
 
 def fill_first(taps, sky, height, w_one):
     spread = (iota((FEAT, LANES), 1) % FEAT == iota((FEAT, LANES), 0)).astype(BF16)
-    rows = dot(taps, spread)
+    rows = [dot(taps[i], spread) for i in range(9)]
     r = iota((8, LANES), 0)
     lane = iota((8, LANES), 1)
     zero = jnp.zeros((8, LANES), F32)
@@ -85,8 +87,8 @@
                     dc = a - bv
                     if 0 <= dc <= 2:
                         for dy in range(3):
-                            tap = (dc * 3 + dy) * 3 + dx
-                            value = jnp.where(masks[bv, dy], rows[tap : tap + 1, :], value)
+                            tap = rows[dc * 3 + dy][dx : dx + 1, :]
+                            value = jnp.where(masks[bv, dy], tap, value)
                 parts.append(value)
             for half in range(5):
                 both = jnp.concatenate([parts[2 * half], parts[2 * half + 1]], axis=0)
@@ -147,7 +149,7 @@
 
     def picked(count, wanted):
         row = iota((lines, count), 0)
-        return (wanted(row // SLAB, row % SLAB) == iota((lines, count), 1)).astype(BF16)
+        return (wanted(row // HEAD, row % HEAD) == iota((lines, count), 1)).astype(BF16)
 
     from_score = picked(ANCHORS, lambda g, k: jnp.where((g == 0) & (k < ANCHORS), k, -1))
     from_box = picked(4 * ANCHORS, lambda g, k: jnp.where((g > 0) & (k < ANCHORS), 4 * k + g - 1, -1))
@@ -179,40 +181,57 @@
         if r not in (3, 4):
             value = jnp.where((y >= 0) & (y < height), value, 0.0)
         lines[CHANS * r : CHANS * (r + 1), :] = value
-    zero = jnp.zeros((8, LANES), F32)
-    for pair in range(PAIRS):
-        both = []
-        for c in (2 * pair - 1, 2 * pair):
-            both.append(lines[pl.ds(c, 8, stride=CHANS), :] if 0 <= c < CHANS else zero)
+    edge = jnp.zeros((16, LANES), BF16)
+    for dx in range(3):
+        shifted[dx, :16, :] = edge
+        for start in range(8 * (CHANS + 2), shifted.shape[1], 16):
+            shifted[dx, start : start + 16, :] = edge
+    for c in range(0, CHANS, 2):
+        both = [lines[pl.ds(c + i, 8, stride=CHANS), :] for i in range(2)]
         for dx in range(3):
             moved = both if dx == 0 else [pltpu.roll(v, LANES - dx, 1) for v in both]
-            shifted[dx, 16 * pair : 16 * pair + 16, :] = jnp.concatenate(moved, axis=0).astype(BF16)
+            shifted[dx, 8 * c + 16 : 8 * c + 32, :] = jnp.concatenate(moved, axis=0).astype(BF16)
 
 
 def convolve_first(shifted, w_one, layer, freq, cols):
-    j = iota((ROWS_ONE, LANES), 0)
-    x = j % SLAB * STRIDE + j // SLAB
+    j = iota((ROWS_ONE, 2 * LANES), 0)
+    lane = iota((ROWS_ONE, 2 * LANES), 1)
+    x = j % 8 * STRIDE + j // SLAB
     col = WIDTH * freq - 2 + x
     inside = (x < WIDTH + 4) & (col >= 0) & (col < cols)
-    turn = ((iota((ROWS_ONE, LANES), 1) == x) & inside).astype(BF16)
+    turn = ((lane == x + j // 8 % 2 * LANES) & inside).astype(BF16)
     zero = jnp.zeros((16, LANES), BF16)
-    edge = jnp.zeros((ROWS_ONE, STEP), BF16)
-    layer[:, :STEP] = edge
-    layer[:, STEP * PAIRS :] = edge
-    for w in range(CHANS // WINDOW):
-        parts = [shifted[dx, 64 * w : 64 * w + 80, :] for dx in range(3)]
-        lhs = dot_nt(turn, jnp.concatenate(parts + [zero], axis=0)).astype(BF16)
-        for n in range(WINDOW_LANES // 256):
-            value = dot(lhs, w_one[:, 256 * n : 256 * n + 256])
-            base = STEP + w * WINDOW_LANES + 256 * n
-            layer[:, base : base + 256] = jnp.maximum(value, 0.0).astype(BF16)
+    blocks = []
+    for w in range(WINDOWS + 1):
+        halves = []
+        for start in (64 * w, 64 * w + 8 * CHANS // 2):
+            parts = [shifted[dx, start : start + 80, :] for dx in range(3)]
+            halves.append(jnp.concatenate(parts + [zero], axis=0))
+        blocks.append(dot_nt(turn, jnp.concatenate(halves, axis=1)).astype(BF16))
+    lhs = jnp.concatenate(blocks, axis=0)
+    row = iota((ROWS_ONE, 256), 0) // 8 % 2
+    lane = iota((ROWS_ONE, 256), 1)
+    for n in range(WINDOW_LANES // 256):
+        count = WINDOWS + 1 if 256 * n < STEP else WINDOWS
+        value = jnp.maximum(dot(lhs[: count * ROWS_ONE], w_one[:, 256 * n : 256 * n + 256]), 0.0)
+        for w in range(count):
+            part = value[ROWS_ONE * w : ROWS_ONE * (w + 1)]
+            base = w * WINDOW_LANES + 256 * n
+            if base == 0:
+                part = jnp.where((row == 0) & (lane < STEP // 2), 0.0, part)
+            if w == WINDOWS:
+                part = jnp.where((row == 1) & (lane >= STEP // 2 - 256 * n), 0.0, part)
+            part = part.astype(BF16)
+            if base + 256 > layer.shape[1]:
+                part = part[:, : layer.shape[1] - base]
+            layer[:, base : base + part.shape[1]] = part
 
 
 def convolve_second(layer, w_two):
     zeroth = jnp.zeros((ROWS_TWO, LANES), F32)
     first = jnp.zeros((ROWS_TWO, LANES), F32)
     for start in range(0, PAIRS, GROUP):
-        pairs = range(start, min(PAIRS, start + GROUP))
+        pairs = range(start, start + GROUP)
         total = None
         for dx in range(3):
             parts = [
@@ -223,47 +242,49 @@
         total = jnp.maximum(total, 0.0)
         for i, p in enumerate(pairs):
             for half in range(2):
-                c = 2 * p - 1 + half
-                if 0 <= c < CHANS:
-                    value = total[
-                        ROWS_TWO * i : ROWS_TWO * (i + 1), LANES * half : LANES * (half + 1)
-                    ]
-                    zeroth = zeroth + value
-                    first = first + ((c + 0.5) / CHANS - 0.5) * value
-    return zeroth * (1.0 / CHANS), first * (12.0 / CHANS)
-
-
-def propose(zeroth, first, w_prop, heads, freq, sky, height, cols, objectness, proposals):
+                c = 2 * p + half
+                value = total[
+                    ROWS_TWO * i : ROWS_TWO * (i + 1), LANES * half : LANES * (half + 1)
+                ]
+                zeroth = zeroth + value
+                first = first + ((c + 0.5) / CHANS - 0.5) * value
+    low, high = [zeroth.reshape(STRIDE, 2, 8, LANES)[:, h].reshape(-1, LANES) for h in range(2)]
+    parts = [first.reshape(STRIDE, 2, 8, LANES)[:, h].reshape(-1, LANES) for h in range(2)]
+    first = parts[0] + parts[1] + 0.5 * high
+    return (low + high) * (1.0 / CHANS), first * (12.0 / CHANS)
+
+
+def propose(zeroth, first, w_prop, heads, freq, sky, height, cols, result):
     maps = jnp.concatenate([zeroth, first], axis=1)
     y = 2 * sky - 1 + iota(maps.shape, 1) // FEAT % 4
     maps = jnp.where((y >= 0) & (y < height), maps, 0.0).astype(BF16)
-    row = iota((3 * WIDTH, ROWS_TWO), 0)
+    row = iota((3 * WIDTH, 8 * STRIDE), 0)
     x = row % WIDTH + row // WIDTH
     col = WIDTH * freq - 1 + x
-    j = iota((3 * WIDTH, ROWS_TWO), 1)
-    turn = ((j % SLAB * STRIDE + j // SLAB == x) & (col >= 0) & (col < cols)).astype(BF16)
+    j = iota((3 * WIDTH, 8 * STRIDE), 1)
+    turn = ((j % 8 * STRIDE + j // 8 == x) & (col >= 0) & (col < cols)).astype(BF16)
     framed = dot(turn, maps).astype(BF16)
     framed = jnp.concatenate([framed[WIDTH * dx : WIDTH * (dx + 1)] for dx in range(3)], axis=1)
     hidden = jnp.maximum(dot(framed, w_prop[...]), 0.0).astype(BF16)
-    k = iota((SLAB, WIDTH), 0)
-    anchor_width = jnp.ones((SLAB, WIDTH), F32)
+    k = iota((HEAD, WIDTH), 0)
+    anchor_width = jnp.ones((HEAD, WIDTH), F32)
     anchor_height = anchor_width
     for anchor in range(ANCHORS):
         scale = 4.0 * 2.0 ** (anchor // 3)
         root = (2.0 ** (anchor % 3 - 1)) ** 0.5
         anchor_width = jnp.where(k == anchor, scale * root, anchor_width)
         anchor_height = jnp.where(k == anchor, scale / root, anchor_height)
-    centre_col = (WIDTH * freq + iota((SLAB, WIDTH), 1)).astype(F32) + 0.5
+    centre_col = (WIDTH * freq + iota((HEAD, WIDTH), 1)).astype(F32) + 0.5
     wide = hidden.shape[1] // 2
     for row in range(2):
         out = dot_nt(heads[...], hidden[:, wide * row : wide * (row + 1)])
-        score, dx, dy, dw, dh = [out[SLAB * g : SLAB * (g + 1)] for g in range(5)]
+        score, dx, dy, dw, dh = [out[HEAD * g : HEAD * (g + 1)] for g in range(5)]
         centre_row = (2 * sky + row).astype(F32) + 0.5
         centre_x = centre_col + dx * anchor_width
         centre_y = centre_row + dy * anchor_height
         half_width = 0.5 * (anchor_width * jnp.exp(dw))
         half_height = 0.5 * (anchor_height * jnp.exp(dh))
-        objectness[:, row, :] = score[:ANCHORS]
+        result[:, 0, row, :] = score[:ANCHORS]
         corners = (
             centre_x - half_width,
             centre_y - half_height,
@@ -271,13 +292,13 @@
             centre_y + half_height,
         )
         for side, corner in enumerate(corners):
-            proposals[:, side, row, :] = (corner * (1.0 / 64.0))[:ANCHORS]
+            result[:, 1 + side, row, :] = (corner * (1.0 / 64.0))[:ANCHORS]
 
 
 def body(
     shape,
     cube_hbm, free_hbm, taps_hbm, kernel_hbm, proposal_hbm, score_hbm, box_hbm,
-    objectness, proposals,
+    result,
     cube, free, taps, kernel, proposal, score, box,
     tx, rx, planes, lines, lines_all, shifted, w_one, spread_taps, w_two, w_prop, heads, layer,
     load_sem, send_sem, recv_sem, halo_send, halo_recv,
@@ -288,18 +309,24 @@
     barrier = pltpu.get_barrier_semaphore()
 
     def freq_peer(i):
-        return {"freq": lax.rem(freq + i, freq_count)}
-
-    def sky_peer(i):
-        return {"sky": lax.rem(sky + i + sky_count, sky_count)}
+        return i + (i >= freq).astype(jnp.int32)
+
+    def in_sky(i):
+        return (sky + i >= 0) & (sky + i < sky_count)
 
     def greet(i, carry):
-        pl.semaphore_signal(barrier, inc=1, device_id=freq_peer(i), device_id_type=MESH)
+        peer = lax.rem(freq + freq_count // 2 + (i + 1) // 2 * (1 - 2 * (i % 2)) + freq_count, freq_count)
+        pl.semaphore_signal(barrier, inc=1, device_id={"freq": peer}, device_id_type=MESH)
         return carry
 
-    lax.fori_loop(1, freq_count, greet, 0)
+    lax.fori_loop(0, freq_count - 1, greet, 0)
+    neighbours = 0
     for i in (-2, -1, 1, 2):
-        pl.semaphore_signal(barrier, inc=1, device_id=sky_peer(i), device_id_type=MESH)
+        neighbours += in_sky(i).astype(jnp.int32)
+
+        @pl.when(in_sky(i))
+        def _():
+            pl.semaphore_signal(barrier, inc=1, device_id={"sky": sky + i}, device_id_type=MESH)
 
     moves = (
         (cube_hbm, cube), (free_hbm, free), (taps_hbm, taps), (kernel_hbm, kernel),
@@ -315,57 +342,73 @@
     loads[1].wait()
     fill_tx(cube, free, tx)
 
-    def exchange(i):
+    def exchange(peer):
         return pltpu.make_async_remote_copy(
-            src_ref=tx.at[lax.rem(freq + i, freq_count)],
+            src_ref=tx.at[peer],
             dst_ref=rx.at[freq],
-            send_sem=send_sem.at[i],
-            recv_sem=recv_sem.at[i],
-            device_id=freq_peer(i),
+            send_sem=send_sem.at[peer],
+            recv_sem=recv_sem.at[freq],
+            device_id={"freq": peer},
             device_id_type=MESH,
         )
 
+    def arrival(peer):
+        return pltpu.make_async_remote_copy(
+            src_ref=tx.at[peer],
+            dst_ref=rx.at[peer],
+            send_sem=send_sem.at[peer],
+            recv_sem=recv_sem.at[peer],
+            device_id={"freq": peer},
+            device_id_type=MESH,
+        )
+
     def send(i, carry):
-        exchange(i).start()
+        exchange(freq_peer(i)).start()
         return carry
 
     def finish(i, carry):
-        exchange(i).wait()
+        arrival(freq_peer(i)).wait_recv()
         return carry
 
-    pl.semaphore_wait(barrier, freq_count + 3)
-    lax.fori_loop(1, freq_count, send, 0)
+    def settle(i, carry):
+        arrival(freq_peer(i)).wait_send()
+        return carry
+
+    pl.semaphore_wait(barrier, freq_count - 1 + neighbours)
+    lax.fori_loop(0, freq_count - 1, send, 0)
     rx[freq] = tx[freq]
     for load in loads[2:]:
         load.wait()
-    fill_first(taps[...], sky, height, w_one)
+    fill_first(taps, sky, height, w_one)
     fill_second(kernel, spread_taps, w_two)
     fill_proposal(proposal, w_prop)
     fill_heads(score, box, heads)
-    lax.fori_loop(1, freq_count, finish, 0)
+    lax.fori_loop(0, freq_count - 1, finish, 0)
 
     flatten(rx, lines, planes, freq, cols)
     halos = []
-    for n, (i, source, target) in enumerate(((1, 3, 1), (-1, 3, 5), (2, 4, 0), (-2, 3, 7))):
+    for n, (i, source, target) in enumerate(((2, 4, 0), (-2, 3, 7), (1, 3, 1), (-1, 3, 5))):
         size = 2 if abs(i) == 1 else 1
-        halos.append(
-            pltpu.make_async_remote_copy(
-                src_ref=planes.at[pl.ds(source, size)],
-                dst_ref=planes.at[pl.ds(target, size)],
-                send_sem=halo_send.at[n],
-                recv_sem=halo_recv.at[n],
-                device_id=sky_peer(i),
-                device_id_type=MESH,
-            )
+        halo = pltpu.make_async_remote_copy(
+            src_ref=planes.at[pl.ds(source, size)],
+            dst_ref=planes.at[pl.ds(target, size)],
+            send_sem=halo_send.at[n],
+            recv_sem=halo_recv.at[n],
+            device_id={"sky": sky + i},
+            device_id_type=MESH,
         )
-    for halo in halos:
-        halo.start()
-    for halo in halos:
-        halo.wait()
+        halos.append((i, halo))
+    for i, halo in halos:
+        pl.when(in_sky(i))(halo.start)
+    for i, halo in halos:
+        pl.when(in_sky(-i))(halo.wait_recv)
     fill_shifted(planes, lines_all, shifted, sky, height)
     convolve_first(shifted, w_one, layer, freq, cols)
     zeroth, first = convolve_second(layer, w_two)
-    propose(zeroth, first, w_prop, heads, freq, sky, height, cols, objectness, proposals)
+    propose(zeroth, first, w_prop, heads, freq, sky, height, cols, result)
+    for i, halo in halos:
+        pl.when(in_sky(i))(halo.wait_send)
+    lax.fori_loop(0, freq_count - 1, settle, 0)
 
 
 def on_device(sky_cube, free_mask, conv_first, conv_second, proposal_conv, score_head, box_head):
@@ -373,7 +416,7 @@
     sky_count = lax.axis_size("sky")
     chans, rows, cols = sky_cube.shape
     wide = proposal_conv.shape[3]
-    taps = conv_first.transpose(1, 2, 3, 4, 0).reshape(27, FEAT)
+    taps = conv_first.transpose(1, 2, 3, 4, 0).reshape(9, 3, FEAT)
     kernel = conv_second.transpose(2, 3, 4, 0, 1).reshape(27, FEAT, FEAT)
     free = free_mask.reshape(1, chans)
     operands = (sky_cube, free, taps, kernel, proposal_conv, score_head, box_head)
@@ -383,12 +426,12 @@
         pltpu.VMEM((8, CHANS, LANES), BF16),
         pltpu.VMEM((2 * CHANS, LANES), F32),
         pltpu.VMEM((8 * CHANS, LANES), F32),
-        pltpu.VMEM((3, 16 * PAIRS, LANES), BF16),
+        pltpu.VMEM((3, 8 * CHANS + 80, LANES), BF16),
         pltpu.VMEM((256, WINDOW_LANES), BF16),
         pltpu.VMEM((27, FEAT, LANES), BF16),
         pltpu.VMEM((3, SPAN, 256), BF16),
         pltpu.VMEM((3 * 256, 2 * wide), BF16),
-        pltpu.VMEM((5 * SLAB, wide), BF16),
+        pltpu.VMEM((5 * HEAD, wide), BF16),
         pltpu.VMEM((ROWS_ONE, STEP * (PAIRS + 1)), BF16),
         pltpu.SemaphoreType.DMA((len(operands),)),
         pltpu.SemaphoreType.DMA((freq_count,)),
@@ -397,19 +440,17 @@
         pltpu.SemaphoreType.DMA((4,)),
     ]
     shape = (freq_count, sky_count, rows * sky_count, cols)
-    return pl.pallas_call(
+    result = pl.pallas_call(
         functools.partial(body, shape),
-        out_shape=(
-            jax.ShapeDtypeStruct((ANCHORS, rows, WIDTH), F32),
-            jax.ShapeDtypeStruct((ANCHORS, 4, rows, WIDTH), F32),
-        ),
-        in_specs=[pl.BlockSpec(memory_space=pl.ANY)] * len(operands),
-        out_specs=(pl.BlockSpec(memory_space=pltpu.VMEM),) * 2,
+        out_shape=pltpu.VMEM((ANCHORS, 5, rows, WIDTH), F32),
+        in_specs=[pl.BlockSpec(memory_space=pltpu.HBM)] * len(operands),
+        out_specs=pl.BlockSpec(memory_space=pltpu.VMEM),
         scratch_shapes=scratch,
         compiler_params=pltpu.CompilerParams(
-            collective_id=0, has_side_effects=True, vmem_limit_bytes=40 * 1024 * 1024
+            collective_id=0, has_side_effects=True, vmem_limit_bytes=60 * 1024 * 1024
         ),
     )(*operands)
+    return result[:, 0], result[:, 1:]
 
 
 def solution(mesh):

time: 42 us -> 34.6 us (0.82)
  the two profiles are of different devices: /device:TPU:4 before, /device:TPU:1 now
where the time goes in v2:
time: 34.6 us; the launch traced here: 34.4 us
  Pallas kernels  32.5 us (94%)
  local copies, waits for them, and re-layouts  1.22 us (4%)
  between operations  0.64 us (2%)
    pallas_call x1, Pallas kernels, on_device(): pl.pallas_call(functools.partial(body, shape), out_shape=pltpu.VMEM((ANCH...  32.5 us

profile of v2, /device:TPU:1, one launch (start us, length us, event | category | flops | bytes accessed | tf_op | source)
XLA Modules:
  0.0 34.4 jit_solution(5809367397145338935)
XLA Ops:
  0.6 32.5 %shard_map.86 = f32[9,5,2,64]{3,2,1,0:T(2,128)S(1)} custom-call(bf16[2,2,2048]{2,1,0:T(2,128)(2,1)} %cube_hbm.1, s32[1,2]{1,0:T(1,128)} %bitcast.11, bf16[9,3,32]{2,1,0:T(4,128)(2,1)} %bitcast.10, bf16[27,32,32]{2,1,0:T(8,128)(2,1)} %bitcast.9, bf16[3,3,64,256]{3,2,1,0:T(8,128)(2,1)} %proposal_hbm.1, bf16[9,256]{1,0:T(8,128)(2,1)} %score_hbm.1, ...), custom_call_target="tpu_custom_call" | custom-call | tf_op jit(solution)/shard_map/pallas_call | solution.py:443
  33.2 0.6 %slice_bitcast_fusion = f32[9,2,64]{2,1,0:T(2,128)} fusion(f32[9,5,2,64]{3,2,1,0:T(2,128)S(1)} %shard_map.86), kind=kLoop, calls=%fused_computation | loop fusion | bytes 9216 | tf_op jit(solution)/shard_map/squeeze | solution.py:453
  33.8 0.6 %slice.7 = f32[9,4,2,64]{3,2,1,0:T(2,128)} slice(f32[9,5,2,64]{3,2,1,0:T(2,128)S(1)} %shard_map.86), slice={[0:9], [1:5], [0:2], [0:64]} | slice | bytes 36864 | tf_op jit(solution)/shard_map/slice | solution.py:453

commit v3 on v2

--- a/solution.py
+++ b/solution.py
@@ -301,12 +301,14 @@
     result,
     cube, free, taps, kernel, proposal, score, box,
     tx, rx, planes, lines, lines_all, shifted, w_one, spread_taps, w_two, w_prop, heads, layer,
-    load_sem, send_sem, recv_sem, halo_send, halo_recv,
+    load_sem, send_sem, recv_sem, halo_send, halo_recv, late, clear,
 ):
     freq_count, sky_count, height, cols = shape
     freq = lax.axis_index("freq")
     sky = lax.axis_index("sky")
     barrier = pltpu.get_barrier_semaphore()
+    cut = freq_count * 6 // 16
+    is_first = freq < cut
 
     def freq_peer(i):
         return i + (i >= freq).astype(jnp.int32)
@@ -319,7 +321,11 @@
         pl.semaphore_signal(barrier, inc=1, device_id={"freq": peer}, device_id_type=MESH)
         return carry
 
-    lax.fori_loop(0, freq_count - 1, greet, 0)
+    @pl.when(is_first)
+    def _():
+        for i in range(freq_count - 1):
+            greet(i, 0)
+
     neighbours = 0
     for i in (-2, -1, 1, 2):
         neighbours += in_sky(i).astype(jnp.int32)
@@ -338,6 +344,17 @@
     ]
     for load in loads:
         load.start()
+    pl.semaphore_wait(barrier, cut - is_first.astype(jnp.int32) + neighbours)
+
+    def announce(i, carry):
+        pl.semaphore_signal(late, inc=1, device_id={"freq": i}, device_id_type=MESH)
+        return carry
+
+    @pl.when(jnp.logical_not(is_first))
+    def _():
+        for i in range(cut):
+            announce(i, 0)
+
     loads[0].wait()
     loads[1].wait()
     fill_tx(cube, free, tx)
@@ -362,20 +379,28 @@
             device_id_type=MESH,
         )
 
-    def send(i, carry):
-        exchange(freq_peer(i)).start()
+    def send(peer):
+        @pl.when(peer != freq)
+        def _():
+            exchange(peer).start()
+
+    def release(i, carry):
+        peer = cut + 2 * i + freq
+        pl.semaphore_signal(clear, inc=1, device_id={"freq": peer}, device_id_type=MESH)
         return carry
 
-    def finish(i, carry):
-        arrival(freq_peer(i)).wait_recv()
-        return carry
-
-    def settle(i, carry):
-        arrival(freq_peer(i)).wait_send()
-        return carry
-
-    pl.semaphore_wait(barrier, freq_count - 1 + neighbours)
-    lax.fori_loop(0, freq_count - 1, send, 0)
+    def finish(i):
+        @pl.when(i != freq)
+        def _():
+            arrival(i).wait_recv()
+
+    def settle(i):
+        @pl.when(i != freq)
+        def _():
+            arrival(i).wait_send()
+
+    for i in range(cut):
+        send(i)
     rx[freq] = tx[freq]
     for load in loads[2:]:
         load.wait()
@@ -383,7 +408,34 @@
     fill_second(kernel, spread_taps, w_two)
     fill_proposal(proposal, w_prop)
     fill_heads(score, box, heads)
-    lax.fori_loop(0, freq_count - 1, finish, 0)
+
+    @pl.when(is_first)
+    def _():
+        pl.semaphore_wait(late, freq_count - cut)
+
+    @pl.when(freq < 2)
+    def _():
+        for i in range((freq_count - cut) // 2):
+            release(i, 0)
+
+    @pl.when(jnp.logical_not(is_first))
+    def _():
+        pl.semaphore_wait(clear, 1)
+
+    from_end = (freq >= freq_count * 3 // 16) & (freq < freq_count * 11 // 16)
+
+    @pl.when(from_end)
+    def _():
+        for i in reversed(range(cut, freq_count)):
+            send(i)
+
+    @pl.when(jnp.logical_not(from_end))
+    def _():
+        for i in range(cut, freq_count):
+            send(i)
+
+    for i in range(freq_count):
+        finish(i)
 
     flatten(rx, lines, planes, freq, cols)
     halos = []
@@ -408,7 +460,8 @@
     propose(zeroth, first, w_prop, heads, freq, sky, height, cols, result)
     for i, halo in halos:
         pl.when(in_sky(i))(halo.wait_send)
-    lax.fori_loop(0, freq_count - 1, settle, 0)
+    for i in range(freq_count):
+        settle(i)
 
 
 def on_device(sky_cube, free_mask, conv_first, conv_second, proposal_conv, score_head, box_head):
@@ -438,6 +491,8 @@
         pltpu.SemaphoreType.DMA((freq_count,)),
         pltpu.SemaphoreType.DMA((4,)),
         pltpu.SemaphoreType.DMA((4,)),
+        pltpu.SemaphoreType.REGULAR,
+        pltpu.SemaphoreType.REGULAR,
     ]
     shape = (freq_count, sky_count, rows * sky_count, cols)
     result = pl.pallas_call(

time: 34.6 us -> 33.5 us (0.968)
  the two profiles are of different devices: /device:TPU:1 before, /device:TPU:491 now
where the time goes in v3:
time: 33.5 us; the launch traced here: 33.3 us
  Pallas kernels  31.4 us (94%)
  local copies, waits for them, and re-layouts  1.22 us (4%)
  between operations  0.64 us (2%)
    pallas_call x1, Pallas kernels, on_device(): pl.pallas_call(functools.partial(body, shape), out_shape=pltpu.VMEM((ANCH...  31.4 us

profile of v3, /device:TPU:491, one launch (start us, length us, event | category | flops | bytes accessed | tf_op | source)
XLA Modules:
  0.0 33.3 jit_solution(14337836686640671562)
XLA Ops:
  0.6 31.4 %shard_map.86 = f32[9,5,2,64]{3,2,1,0:T(2,128)S(1)} custom-call(bf16[2,2,2048]{2,1,0:T(2,128)(2,1)} %cube_hbm.1, s32[1,2]{1,0:T(1,128)} %bitcast.11, bf16[9,3,32]{2,1,0:T(4,128)(2,1)} %bitcast.10, bf16[27,32,32]{2,1,0:T(8,128)(2,1)} %bitcast.9, bf16[3,3,64,256]{3,2,1,0:T(8,128)(2,1)} %proposal_hbm.1, bf16[9,256]{1,0:T(8,128)(2,1)} %score_hbm.1, ...), custom_call_target="tpu_custom_call" | custom-call | tf_op jit(solution)/shard_map/pallas_call | solution.py:498
  32.1 0.6 %slice_bitcast_fusion = f32[9,2,64]{2,1,0:T(2,128)} fusion(f32[9,5,2,64]{3,2,1,0:T(2,128)S(1)} %shard_map.86), kind=kLoop, calls=%fused_computation | loop fusion | bytes 9216 | tf_op jit(solution)/shard_map/squeeze | solution.py:508
  32.7 0.6 %slice.7 = f32[9,4,2,64]{3,2,1,0:T(2,128)} slice(f32[9,5,2,64]{3,2,1,0:T(2,128)S(1)} %shard_map.86), slice={[0:9], [1:5], [0:2], [0:64]} | slice | bytes 36864 | tf_op jit(solution)/shard_map/slice | solution.py:508

commit v4 on v3

--- a/solution.py
+++ b/solution.py
@@ -21,10 +21,9 @@
 ROWS_ONE = (STRIDE + 2) * SLAB
 ROWS_TWO = STRIDE * SLAB
 PAIRS = CHANS // 4
-STEP = 2 * 6 * FEAT
-SPAN = 2 * STEP
+EARLY = 2
+LATE = 4
 WINDOW = 8
-WINDOW_LANES = WINDOW * 6 * FEAT
 WINDOWS = CHANS // 2 // WINDOW
 GROUP = 4
 NT = (((1,), (1,)), ((), ()))
@@ -61,43 +60,64 @@
         tx[block] = jnp.where(lane == LANES - 1, marks, piece).astype(BF16)
 
 
-def fill_first(taps, sky, height, w_one):
+def late_row(index, odd):
+    return index + 2 * (index >= jnp.where(odd, 1, 3)).astype(jnp.int32)
+
+
+def fill_first(taps, sky, height, odd, w_early, w_late):
     spread = (iota((FEAT, LANES), 1) % FEAT == iota((FEAT, LANES), 0)).astype(BF16)
     rows = [dot(taps[i], spread) for i in range(9)]
-    r = iota((8, LANES), 0)
+    sub = iota((8, LANES), 0)
     lane = iota((8, LANES), 1)
     zero = jnp.zeros((8, LANES), F32)
-    for tile in range(WINDOW_LANES // LANES):
-        block = 4 * tile + lane // FEAT
-        q = block % 6
-        b = block // 6
-        y = 2 * sky - 2 + q
-        inside = (y >= 0) & (y < height)
-        row_masks = [(r - q == dy) & inside for dy in range(3)]
-        b_values = sorted({(4 * tile) // 6, (4 * tile + 3) // 6})
-        masks = {}
-        for bv in b_values:
-            for dy in range(3):
-                masks[bv, dy] = row_masks[dy] & (b == bv) if len(b_values) > 1 else row_masks[dy]
+
+    def store(target, base, tile, parts):
+        for half in range(len(parts) // 2):
+            both = jnp.concatenate([parts[2 * half], parts[2 * half + 1]], axis=0)
+            start = base + 16 * half
+            target[start : start + 16, tile * LANES : (tile + 1) * LANES] = both.astype(BF16)
+
+    step_rows = [sub % 4 - lane // FEAT % 2 == dy for dy in range(3)]
+    apart = sub // 4 - lane // (2 * FEAT)
+    masks = {}
+    for shift in range(-1, 4):
+        for dc in range(3):
+            if -1 <= dc - shift <= 1:
+                for dy in range(3):
+                    masks[shift, dc, dy] = step_rows[dy] & (apart == dc - shift)
+    for tile in range(WINDOW * EARLY * FEAT // LANES):
+        for dx in range(3):
+            parts = []
+            for pair in range(6):
+                value = zero
+                for dc in range(3):
+                    for dy in range(3):
+                        mask = masks.get((2 * pair - 2 * tile, dc, dy))
+                        if mask is not None:
+                            value = jnp.where(mask, rows[dc * 3 + dy][dx : dx + 1, :], value)
+                parts.append(value)
+            store(w_early, 48 * dx, tile, parts)
+        w_early[144:256, tile * LANES : (tile + 1) * LANES] = jnp.zeros((112, LANES), BF16)
+
+    q = late_row(lane // FEAT, odd)
+    y = 2 * sky - 2 + q
+    inside = (y >= 0) & (y < height)
+    row_masks = [(sub - q == dy) & inside for dy in range(3)]
+    for tile in range(WINDOW):
         for dx in range(3):
             parts = []
             for a in range(10):
                 value = zero
-                for bv in b_values:
-                    dc = a - bv
-                    if 0 <= dc <= 2:
-                        for dy in range(3):
-                            tap = rows[dc * 3 + dy][dx : dx + 1, :]
-                            value = jnp.where(masks[bv, dy], tap, value)
+                dc = a - tile
+                if 0 <= dc <= 2:
+                    for dy in range(3):
+                        value = jnp.where(row_masks[dy], rows[dc * 3 + dy][dx : dx + 1, :], value)
                 parts.append(value)
-            for half in range(5):
-                both = jnp.concatenate([parts[2 * half], parts[2 * half + 1]], axis=0)
-                base = 80 * dx + 16 * half
-                w_one[base : base + 16, tile * LANES : (tile + 1) * LANES] = both.astype(BF16)
-        w_one[240:256, tile * LANES : (tile + 1) * LANES] = jnp.zeros((16, LANES), BF16)
-
-
-def fill_second(kernel, spread_taps, w_two):
+            store(w_late, 80 * dx, tile, parts)
+        w_late[240:256, tile * LANES : (tile + 1) * LANES] = jnp.zeros((16, LANES), BF16)
+
+
+def fill_second(kernel, odd, spread_taps, w_early, w_late):
     eye = (iota((FEAT, FEAT), 0) == iota((FEAT, FEAT), 1)).astype(BF16)
     source = iota((LANES, 4 * LANES), 0)
     target = iota((LANES, 4 * LANES), 1)
@@ -111,22 +131,30 @@
         wide = dot(turned, spread).astype(BF16)
         for g in range(count):
             spread_taps[4 * t + g] = wide[:, g * LANES : (g + 1) * LANES]
-    group = iota((FEAT, LANES), 1) // FEAT
+    lane = iota((FEAT, LANES), 1) // FEAT
     zero = jnp.zeros((FEAT, LANES), BF16)
+
+    def block(dx, dc, offset):
+        value = zero
+        if 0 <= dc <= 2:
+            for dy in range(3):
+                tap = spread_taps[(dc * 3 + dy) * 3 + dx]
+                value = jnp.where(lane == offset - dy, tap, value)
+        return value
+
     for dx in range(3):
         for cin in range(4):
-            for yin in range(6):
-                base = (cin * 6 + yin) * FEAT
-                for cout in range(2):
-                    value = zero
-                    dc = cin - cout
-                    if 0 <= dc <= 2:
-                        for yout in range(4):
-                            dy = yin - yout
-                            if 0 <= dy <= 2:
-                                tap = spread_taps[(dc * 3 + dy) * 3 + dx]
-                                value = jnp.where(group == yout, tap, value)
-                    w_two[dx, base : base + FEAT, cout * LANES : (cout + 1) * LANES] = value
+            for cout in range(2):
+                lanes = slice(cout * LANES, (cout + 1) * LANES)
+                for e in range(EARLY):
+                    base = (cin * EARLY + e) * FEAT
+                    q = jnp.where(odd, 1, 3) + e
+                    w_early[dx, base : base + FEAT, lanes] = block(dx, cin - cout, q)
+                for l in range(LATE):
+                    base = (cin * LATE + l) * FEAT
+                    w_late[dx, base : base + FEAT, lanes] = block(
+                        dx, cin - cout, late_row(jnp.int32(l), odd)
+                    )
 
 
 def fill_proposal(kernel, w_prop):
@@ -174,72 +202,78 @@
         planes[3 + y] = lines[pl.ds(y, CHANS, stride=2), :].astype(BF16)
 
 
-def fill_shifted(planes, lines, shifted, sky, height):
-    for r in range(8):
-        y = 2 * sky - 3 + r
-        value = planes[r].astype(F32)
-        if r not in (3, 4):
-            value = jnp.where((y >= 0) & (y < height), value, 0.0)
-        lines[CHANS * r : CHANS * (r + 1), :] = value
-    edge = jnp.zeros((16, LANES), BF16)
-    for dx in range(3):
-        shifted[dx, :16, :] = edge
-        for start in range(8 * (CHANS + 2), shifted.shape[1], 16):
-            shifted[dx, start : start + 16, :] = edge
-    for c in range(0, CHANS, 2):
-        both = [lines[pl.ds(c + i, 8, stride=CHANS), :] for i in range(2)]
+def shift_columns(lines, shifted):
+    for start in range(0, lines.shape[0], 16):
+        part = lines[start : start + 16, :]
         for dx in range(3):
-            moved = both if dx == 0 else [pltpu.roll(v, LANES - dx, 1) for v in both]
-            shifted[dx, 8 * c + 16 : 8 * c + 32, :] = jnp.concatenate(moved, axis=0).astype(BF16)
-
-
-def convolve_first(shifted, w_one, layer, freq, cols):
+            moved = part if dx == 0 else pltpu.roll(part, LANES - dx, 1)
+            shifted[dx, start : start + 16, :] = moved.astype(BF16)
+
+
+def clear_edges(lines, count):
+    for start, stop in ((0, 2 * count), ((CHANS + 2) * count, lines.shape[0])):
+        lines[start:stop, :] = jnp.zeros((stop - start, LANES), F32)
+
+
+def columns_to_rows(shifted, count, span, freq, cols):
     j = iota((ROWS_ONE, 2 * LANES), 0)
     lane = iota((ROWS_ONE, 2 * LANES), 1)
     x = j % 8 * STRIDE + j // SLAB
     col = WIDTH * freq - 2 + x
     inside = (x < WIDTH + 4) & (col >= 0) & (col < cols)
     turn = ((lane == x + j // 8 % 2 * LANES) & inside).astype(BF16)
-    zero = jnp.zeros((16, LANES), BF16)
+    zero = jnp.zeros((256 - 3 * span, LANES), BF16)
     blocks = []
     for w in range(WINDOWS + 1):
         halves = []
-        for start in (64 * w, 64 * w + 8 * CHANS // 2):
-            parts = [shifted[dx, start : start + 80, :] for dx in range(3)]
+        for start in (WINDOW * count * w, WINDOW * count * w + count * CHANS // 2):
+            parts = [shifted[dx, start : start + span, :] for dx in range(3)]
             halves.append(jnp.concatenate(parts + [zero], axis=0))
         blocks.append(dot_nt(turn, jnp.concatenate(halves, axis=1)).astype(BF16))
-    lhs = jnp.concatenate(blocks, axis=0)
+    return jnp.concatenate(blocks, axis=0)
+
+
+def convolve_first(lhs, weights, layer):
+    lanes = weights.shape[1]
+    chan = lanes // WINDOW
+    tail = layer.shape[1] - WINDOWS * lanes
     row = iota((ROWS_ONE, 256), 0) // 8 % 2
     lane = iota((ROWS_ONE, 256), 1)
-    for n in range(WINDOW_LANES // 256):
-        count = WINDOWS + 1 if 256 * n < STEP else WINDOWS
-        value = jnp.maximum(dot(lhs[: count * ROWS_ONE], w_one[:, 256 * n : 256 * n + 256]), 0.0)
+    for n in range(lanes // 256):
+        count = WINDOWS + 1 if 256 * n < tail else WINDOWS
+        value = jnp.maximum(dot(lhs[: count * ROWS_ONE], weights[:, 256 * n : 256 * n + 256]), 0.0)
         for w in range(count):
             part = value[ROWS_ONE * w : ROWS_ONE * (w + 1)]
-            base = w * WINDOW_LANES + 256 * n
+            base = w * lanes + 256 * n
             if base == 0:
-                part = jnp.where((row == 0) & (lane < STEP // 2), 0.0, part)
+                part = jnp.where((row == 0) & (lane < chan), 0.0, part)
             if w == WINDOWS:
-                part = jnp.where((row == 1) & (lane >= STEP // 2 - 256 * n), 0.0, part)
-            part = part.astype(BF16)
-            if base + 256 > layer.shape[1]:
-                part = part[:, : layer.shape[1] - base]
+                part = jnp.where((row == 1) & (lane >= chan - 256 * n), 0.0, part)
+            part = part[:, : min(256, layer.shape[1] - base)].astype(BF16)
             layer[:, base : base + part.shape[1]] = part
 
 
-def convolve_second(layer, w_two):
+def convolve_second(layer, weights, pairs):
+    span = weights.shape[1]
+    step = span // 2
+    total = None
+    for dx in range(3):
+        parts = [layer[SLAB * dx : SLAB * dx + ROWS_TWO, step * p : step * p + span] for p in pairs]
+        part = dot(jnp.concatenate(parts, axis=0), weights[dx])
+        total = part if total is None else total + part
+    return total
+
+
+def groups():
+    return [range(start, start + GROUP) for start in range(0, PAIRS, GROUP)]
+
+
+def sum_moments(layer, weights, partial):
     zeroth = jnp.zeros((ROWS_TWO, LANES), F32)
     first = jnp.zeros((ROWS_TWO, LANES), F32)
-    for start in range(0, PAIRS, GROUP):
-        pairs = range(start, start + GROUP)
-        total = None
-        for dx in range(3):
-            parts = [
-                layer[SLAB * dx : SLAB * dx + ROWS_TWO, STEP * p : STEP * p + SPAN] for p in pairs
-            ]
-            part = dot(jnp.concatenate(parts, axis=0), w_two[dx])
-            total = part if total is None else total + part
-        total = jnp.maximum(total, 0.0)
+    for pairs in groups():
+        rows = pl.ds(pairs[0] * ROWS_TWO, GROUP * ROWS_TWO)
+        total = jnp.maximum(convolve_second(layer, weights, pairs) + partial[rows, :], 0.0)
         for i, p in enumerate(pairs):
             for half in range(2):
                 c = 2 * p + half
@@ -300,14 +334,16 @@
     cube_hbm, free_hbm, taps_hbm, kernel_hbm, proposal_hbm, score_hbm, box_hbm,
     result,
     cube, free, taps, kernel, proposal, score, box,
-    tx, rx, planes, lines, lines_all, shifted, w_one, spread_taps, w_two, w_prop, heads, layer,
+    tx, rx, planes, lines, lines_early, lines_late, shifted_early, shifted_late, w_one_early, w_one_late,
+    spread_taps, w_two_early, w_two_late, w_prop, heads, layer_early, layer_late, partial,
     load_sem, send_sem, recv_sem, halo_send, halo_recv, late, clear,
 ):
     freq_count, sky_count, height, cols = shape
     freq = lax.axis_index("freq")
     sky = lax.axis_index("sky")
+    odd = lax.rem(sky, 2) == 1
     barrier = pltpu.get_barrier_semaphore()
-    cut = freq_count * 6 // 16
+    cut = max(2, freq_count * 3 // 8 // 2 * 2)
     is_first = freq < cut
 
     def freq_peer(i):
@@ -404,10 +440,12 @@
     rx[freq] = tx[freq]
     for load in loads[2:]:
         load.wait()
-    fill_first(taps, sky, height, w_one)
-    fill_second(kernel, spread_taps, w_two)
+    fill_first(taps, sky, height, odd, w_one_early, w_one_late)
+    fill_second(kernel, odd, spread_taps, w_two_early, w_two_late)
     fill_proposal(proposal, w_prop)
     fill_heads(score, box, heads)
+    clear_edges(lines_early, 4)
+    clear_edges(lines_late, 8)
 
     @pl.when(is_first)
     def _():
@@ -452,11 +490,33 @@
         halos.append((i, halo))
     for i, halo in halos:
         pl.when(in_sky(i))(halo.start)
+    mate = dict(halos)
+    pl.when(odd)(mate[1].wait_recv)
+    pl.when(jnp.logical_not(odd))(mate[-1].wait_recv)
+    for i in range(4):
+        lines_early[pl.ds(8 + i, CHANS, stride=4), :] = planes[jnp.where(odd, 1, 3) + i].astype(F32)
+    shift_columns(lines_early, shifted_early)
+    convolve_first(
+        columns_to_rows(shifted_early, 4, 48, freq, cols), w_one_early, layer_early
+    )
+    for pairs in groups():
+        rows = pl.ds(pairs[0] * ROWS_TWO, GROUP * ROWS_TWO)
+        partial[rows, :] = convolve_second(layer_early, w_two_early, pairs)
+
     for i, halo in halos:
-        pl.when(in_sky(-i))(halo.wait_recv)
-    fill_shifted(planes, lines_all, shifted, sky, height)
-    convolve_first(shifted, w_one, layer, freq, cols)
-    zeroth, first = convolve_second(layer, w_two)
+        if abs(i) == 2:
+            pl.when(in_sky(-i))(halo.wait_recv)
+    pl.when(jnp.logical_not(odd) & in_sky(-1))(mate[1].wait_recv)
+    pl.when(odd & in_sky(1))(mate[-1].wait_recv)
+    for r in range(8):
+        y = 2 * sky - 3 + r
+        value = planes[r].astype(F32)
+        if r not in (3, 4):
+            value = jnp.where((y >= 0) & (y < height), value, 0.0)
+        lines_late[pl.ds(16 + r, CHANS, stride=8), :] = value
+    shift_columns(lines_late, shifted_late)
+    convolve_first(columns_to_rows(shifted_late, 8, 80, freq, cols), w_one_late, layer_late)
+    zeroth, first = sum_moments(layer_late, w_two_late, partial)
     propose(zeroth, first, w_prop, heads, freq, sky, height, cols, result)
     for i, halo in halos:
         pl.when(in_sky(i))(halo.wait_send)
@@ -478,14 +538,20 @@
         pltpu.VMEM((freq_count, chans * rows, LANES), BF16),
         pltpu.VMEM((8, CHANS, LANES), BF16),
         pltpu.VMEM((2 * CHANS, LANES), F32),
-        pltpu.VMEM((8 * CHANS, LANES), F32),
+        pltpu.VMEM((4 * CHANS + 48, LANES), F32),
+        pltpu.VMEM((8 * CHANS + 80, LANES), F32),
+        pltpu.VMEM((3, 4 * CHANS + 48, LANES), BF16),
         pltpu.VMEM((3, 8 * CHANS + 80, LANES), BF16),
-        pltpu.VMEM((256, WINDOW_LANES), BF16),
+        pltpu.VMEM((256, WINDOW * EARLY * FEAT), BF16),
+        pltpu.VMEM((256, WINDOW * LATE * FEAT), BF16),
         pltpu.VMEM((27, FEAT, LANES), BF16),
-        pltpu.VMEM((3, SPAN, 256), BF16),
+        pltpu.VMEM((3, 4 * EARLY * FEAT, 256), BF16),
+        pltpu.VMEM((3, 4 * LATE * FEAT, 256), BF16),
         pltpu.VMEM((3 * 256, 2 * wide), BF16),
         pltpu.VMEM((5 * HEAD, wide), BF16),
-        pltpu.VMEM((ROWS_ONE, STEP * (PAIRS + 1)), BF16),
+        pltpu.VMEM((ROWS_ONE, 2 * (PAIRS + 1) * EARLY * FEAT), BF16),
+        pltpu.VMEM((ROWS_ONE, 2 * (PAIRS + 1) * LATE * FEAT), BF16),
+        pltpu.VMEM((PAIRS * ROWS_TWO, 256), F32),
         pltpu.SemaphoreType.DMA((len(operands),)),
         pltpu.SemaphoreType.DMA((freq_count,)),
         pltpu.SemaphoreType.DMA((freq_count,)),

time: 33.5 us -> 32.4 us (0.967)
  Pallas kernels: 31.4 us -> 30.3 us
    pallas_call x1, Pallas kernels: 31.4 us -> 30.3 us  [on_device(): pl.pallas_call(functools.partial(body, shape), out_shape=pltpu.VMEM((ANCH...]
where the time goes in v4:
time: 32.4 us; the launch traced here: 32.2 us
  Pallas kernels  30.3 us (94%)
  local copies, waits for them, and re-layouts  1.22 us (4%)
  between operations  0.64 us (2%)
    pallas_call x1, Pallas kernels, on_device(): pl.pallas_call(functools.partial(body, shape), out_shape=pltpu.VMEM((ANCH...  30.3 us

profile of v4, /device:TPU:491, one launch (start us, length us, event | category | flops | bytes accessed | tf_op | source)
XLA Modules:
  0.0 32.2 jit_solution(17289394832111958201)
XLA Ops:
  0.6 30.3 %shard_map.86 = f32[9,5,2,64]{3,2,1,0:T(2,128)S(1)} custom-call(bf16[2,2,2048]{2,1,0:T(2,128)(2,1)} %cube_hbm.1, s32[1,2]{1,0:T(1,128)} %bitcast.11, bf16[9,3,32]{2,1,0:T(4,128)(2,1)} %bitcast.10, bf16[27,32,32]{2,1,0:T(8,128)(2,1)} %bitcast.9, bf16[3,3,64,256]{3,2,1,0:T(8,128)(2,1)} %proposal_hbm.1, bf16[9,256]{1,0:T(8,128)(2,1)} %score_hbm.1, ...), custom_call_target="tpu_custom_call" | custom-call | tf_op jit(solution)/shard_map/pallas_call | solution.py:564
  31.0 0.6 %slice_bitcast_fusion = f32[9,2,64]{2,1,0:T(2,128)} fusion(f32[9,5,2,64]{3,2,1,0:T(2,128)S(1)} %shard_map.86), kind=kLoop, calls=%fused_computation | loop fusion | bytes 9216 | tf_op jit(solution)/shard_map/squeeze | solution.py:574
  31.6 0.6 %slice.7 = f32[9,4,2,64]{3,2,1,0:T(2,128)} slice(f32[9,5,2,64]{3,2,1,0:T(2,128)S(1)} %shard_map.86), slice={[0:9], [1:5], [0:2], [0:64]} | slice | bytes 36864 | tf_op jit(solution)/shard_map/slice | solution.py:574

commit v5 on v4

--- a/solution.py
+++ b/solution.py
@@ -337,14 +337,23 @@
     tx, rx, planes, lines, lines_early, lines_late, shifted_early, shifted_late, w_one_early, w_one_late,
     spread_taps, w_two_early, w_two_late, w_prop, heads, layer_early, layer_late, partial,
     load_sem, send_sem, recv_sem, halo_send, halo_recv, late, clear,
+    passing, hub_send, hub_recv,
 ):
     freq_count, sky_count, height, cols = shape
     freq = lax.axis_index("freq")
     sky = lax.axis_index("sky")
     odd = lax.rem(sky, 2) == 1
     barrier = pltpu.get_barrier_semaphore()
-    cut = max(2, freq_count * 3 // 8 // 2 * 2)
+    cut = max(2, freq_count * 7 // 16 // 2 * 2)
     is_first = freq < cut
+    middle = freq_count * 11 // 16
+    end = freq_count * 3 // 4
+    hubs = (freq_count - end) // 2
+    is_source = (freq >= cut) & (freq < middle)
+    is_hub = (freq >= 2) & (freq < 2 + 2 * hubs)
+
+    def hub_of(target):
+        return 2 * (hubs - (target - end) // 2) + target % 2
 
     def freq_peer(i):
         return i + (i >= freq).astype(jnp.int32)
@@ -416,9 +425,43 @@
         )
 
     def send(peer):
-        @pl.when(peer != freq)
+        wanted = peer != freq
+        if peer >= end:
+            wanted &= jnp.logical_not(is_source)
+
+        @pl.when(wanted)
         def _():
             exchange(peer).start()
+
+    def to_hub(peer):
+        return pltpu.make_async_remote_copy(
+            src_ref=tx.at[peer],
+            dst_ref=passing.at[freq - cut],
+            send_sem=send_sem.at[peer],
+            recv_sem=hub_recv.at[freq - cut],
+            device_id={"freq": hub_of(peer)},
+            device_id_type=MESH,
+        )
+
+    def from_hub(slot):
+        return pltpu.make_async_remote_copy(
+            src_ref=passing.at[slot],
+            dst_ref=rx.at[cut + slot],
+            send_sem=hub_send.at[slot],
+            recv_sem=recv_sem.at[cut + slot],
+            device_id={"freq": end + 2 * (hubs - freq // 2) + lax.rem(freq, 2)},
+            device_id_type=MESH,
+        )
+
+    def at_hub(slot):
+        return pltpu.make_async_remote_copy(
+            src_ref=passing.at[slot],
+            dst_ref=passing.at[slot],
+            send_sem=hub_send.at[slot],
+            recv_sem=hub_recv.at[slot],
+            device_id={"freq": cut + slot},
+            device_id_type=MESH,
+        )
 
     def release(i, carry):
         peer = cut + 2 * i + freq
@@ -437,6 +480,12 @@
 
     for i in range(cut):
         send(i)
+
+    @pl.when(is_source)
+    def _():
+        for peer in reversed(range(end, freq_count)):
+            to_hub(peer).start()
+
     rx[freq] = tx[freq]
     for load in loads[2:]:
         load.wait()
@@ -471,6 +520,12 @@
     def _():
         for i in range(cut, freq_count):
             send(i)
+
+    @pl.when(is_hub)
+    def _():
+        for slot in range(middle - cut):
+            at_hub(slot).wait_recv()
+            from_hub(slot).start()
 
     for i in range(freq_count):
         finish(i)
@@ -504,6 +559,16 @@
         partial[rows, :] = convolve_second(layer_early, w_two_early, pairs)
 
     for i, halo in halos:
+        pl.when(in_sky(i))(halo.wait_send)
+    for i in range(freq_count):
+        settle(i)
+
+    @pl.when(is_hub)
+    def _():
+        for slot in range(middle - cut):
+            from_hub(slot).wait_send()
+
+    for i, halo in halos:
         if abs(i) == 2:
             pl.when(in_sky(-i))(halo.wait_recv)
     pl.when(jnp.logical_not(odd) & in_sky(-1))(mate[1].wait_recv)
@@ -518,10 +583,6 @@
     convolve_first(columns_to_rows(shifted_late, 8, 80, freq, cols), w_one_late, layer_late)
     zeroth, first = sum_moments(layer_late, w_two_late, partial)
     propose(zeroth, first, w_prop, heads, freq, sky, height, cols, result)
-    for i, halo in halos:
-        pl.when(in_sky(i))(halo.wait_send)
-    for i in range(freq_count):
-        settle(i)
 
 
 def on_device(sky_cube, free_mask, conv_first, conv_second, proposal_conv, score_head, box_head):
@@ -559,6 +620,9 @@
         pltpu.SemaphoreType.DMA((4,)),
         pltpu.SemaphoreType.REGULAR,
         pltpu.SemaphoreType.REGULAR,
+        pltpu.VMEM((freq_count // 4, chans * rows, LANES), BF16),
+        pltpu.SemaphoreType.DMA((freq_count // 4,)),
+        pltpu.SemaphoreType.DMA((freq_count // 4,)),
     ]
     shape = (freq_count, sky_count, rows * sky_count, cols)
     result = pl.pallas_call(

time: 32.4 us -> 31.6 us (0.975)
  the two profiles are of different devices: /device:TPU:491 before, /device:TPU:459 now
where the time goes in v5:
time: 31.6 us; the launch traced here: 31.4 us
  Pallas kernels  29.5 us (93%)
  local copies, waits for them, and re-layouts  1.22 us (4%)
  between operations  0.64 us (2%)
    pallas_call x1, Pallas kernels, on_device(): pl.pallas_call(functools.partial(body, shape), out_shape=pltpu.VMEM((ANCH...  29.5 us

profile of v5, /device:TPU:459, one launch (start us, length us, event | category | flops | bytes accessed | tf_op | source)
XLA Modules:
  0.0 31.4 jit_solution(13314517712630807108)
XLA Ops:
  0.6 29.5 %shard_map.86 = f32[9,5,2,64]{3,2,1,0:T(2,128)S(1)} custom-call(bf16[2,2,2048]{2,1,0:T(2,128)(2,1)} %cube_hbm.1, s32[1,2]{1,0:T(1,128)} %bitcast.11, bf16[9,3,32]{2,1,0:T(4,128)(2,1)} %bitcast.10, bf16[27,32,32]{2,1,0:T(8,128)(2,1)} %bitcast.9, bf16[3,3,64,256]{3,2,1,0:T(8,128)(2,1)} %proposal_hbm.1, bf16[9,256]{1,0:T(8,128)(2,1)} %score_hbm.1, ...), custom_call_target="tpu_custom_call" | custom-call | tf_op jit(solution)/shard_map/pallas_call | solution.py:628
  30.2 0.6 %slice_bitcast_fusion = f32[9,2,64]{2,1,0:T(2,128)} fusion(f32[9,5,2,64]{3,2,1,0:T(2,128)S(1)} %shard_map.86), kind=kLoop, calls=%fused_computation | loop fusion | bytes 9216 | tf_op jit(solution)/shard_map/squeeze | solution.py:638
  30.8 0.6 %slice.7 = f32[9,4,2,64]{3,2,1,0:T(2,128)} slice(f32[9,5,2,64]{3,2,1,0:T(2,128)S(1)} %shard_map.86), slice={[0:9], [1:5], [0:2], [0:64]} | slice | bytes 36864 | tf_op jit(solution)/shard_map/slice | solution.py:638

commit v6 on v5

--- a/solution.py
+++ b/solution.py
@@ -41,7 +41,7 @@
     return lax.dot_general(a, b, NT, preferred_element_type=F32)
 
 
-def fill_tx(cube, free, tx):
+def fill_tx(cube, free, tx, count, send):
     chans, rows, cols = cube.shape
     lines = chans * rows
     values = cube[...].astype(F32).reshape(lines, cols)
@@ -58,6 +58,9 @@
         start = block // 2 * LANES
         piece = source[:, start : start + LANES]
         tx[block] = jnp.where(lane == LANES - 1, marks, piece).astype(BF16)
+        if block == count - 1:
+            for peer in range(count):
+                send(peer)
 
 
 def late_row(index, odd):
@@ -300,33 +303,33 @@
     framed = dot(turn, maps).astype(BF16)
     framed = jnp.concatenate([framed[WIDTH * dx : WIDTH * (dx + 1)] for dx in range(3)], axis=1)
     hidden = jnp.maximum(dot(framed, w_prop[...]), 0.0).astype(BF16)
-    k = iota((HEAD, WIDTH), 0)
-    anchor_width = jnp.ones((HEAD, WIDTH), F32)
+    wide = hidden.shape[1] // 2
+    stacked = jnp.concatenate([hidden[:, :wide], hidden[:, wide:]], axis=0)
+    out = dot_nt(heads[...], stacked)
+    score, dx, dy, dw, dh = [out[HEAD * g : HEAD * (g + 1)] for g in range(5)]
+    k = iota(score.shape, 0)
+    lane = iota(score.shape, 1)
+    anchor_width = jnp.ones(score.shape, F32)
     anchor_height = anchor_width
     for anchor in range(ANCHORS):
         scale = 4.0 * 2.0 ** (anchor // 3)
         root = (2.0 ** (anchor % 3 - 1)) ** 0.5
         anchor_width = jnp.where(k == anchor, scale * root, anchor_width)
         anchor_height = jnp.where(k == anchor, scale / root, anchor_height)
-    centre_col = (WIDTH * freq + iota((HEAD, WIDTH), 1)).astype(F32) + 0.5
-    wide = hidden.shape[1] // 2
-    for row in range(2):
-        out = dot_nt(heads[...], hidden[:, wide * row : wide * (row + 1)])
-        score, dx, dy, dw, dh = [out[HEAD * g : HEAD * (g + 1)] for g in range(5)]
-        centre_row = (2 * sky + row).astype(F32) + 0.5
-        centre_x = centre_col + dx * anchor_width
-        centre_y = centre_row + dy * anchor_height
-        half_width = 0.5 * (anchor_width * jnp.exp(dw))
-        half_height = 0.5 * (anchor_height * jnp.exp(dh))
-        result[:, 0, row, :] = score[:ANCHORS]
-        corners = (
-            centre_x - half_width,
-            centre_y - half_height,
-            centre_x + half_width,
-            centre_y + half_height,
-        )
-        for side, corner in enumerate(corners):
-            result[:, 1 + side, row, :] = (corner * (1.0 / 64.0))[:ANCHORS]
+    centre_x = (WIDTH * freq + lane % WIDTH).astype(F32) + 0.5 + dx * anchor_width
+    centre_y = (2 * sky + lane // WIDTH).astype(F32) + 0.5 + dy * anchor_height
+    half_width = 0.5 * (anchor_width * jnp.exp(dw))
+    half_height = 0.5 * (anchor_height * jnp.exp(dh))
+    corners = (
+        centre_x - half_width,
+        centre_y - half_height,
+        centre_x + half_width,
+        centre_y + half_height,
+    )
+    parts = (score,) + tuple(corner * (1.0 / 64.0) for corner in corners)
+    for g, part in enumerate(parts):
+        for row in range(2):
+            result[:, g, row, :] = part[:ANCHORS, WIDTH * row : WIDTH * (row + 1)]
 
 
 def body(
@@ -349,7 +352,8 @@
     middle = freq_count * 11 // 16
     end = freq_count * 3 // 4
     hubs = (freq_count - end) // 2
-    is_source = (freq >= cut) & (freq < middle)
+    origin = min(cut, 2 + 2 * hubs)
+    is_source = (freq >= origin) & (freq < middle)
     is_hub = (freq >= 2) & (freq < 2 + 2 * hubs)
 
     def hub_of(target):
@@ -365,19 +369,6 @@
         peer = lax.rem(freq + freq_count // 2 + (i + 1) // 2 * (1 - 2 * (i % 2)) + freq_count, freq_count)
         pl.semaphore_signal(barrier, inc=1, device_id={"freq": peer}, device_id_type=MESH)
         return carry
-
-    @pl.when(is_first)
-    def _():
-        for i in range(freq_count - 1):
-            greet(i, 0)
-
-    neighbours = 0
-    for i in (-2, -1, 1, 2):
-        neighbours += in_sky(i).astype(jnp.int32)
-
-        @pl.when(in_sky(i))
-        def _():
-            pl.semaphore_signal(barrier, inc=1, device_id={"sky": sky + i}, device_id_type=MESH)
 
     moves = (
         (cube_hbm, cube), (free_hbm, free), (taps_hbm, taps), (kernel_hbm, kernel),
@@ -387,7 +378,23 @@
         pltpu.make_async_copy(source, target, load_sem.at[i])
         for i, (source, target) in enumerate(moves)
     ]
-    for load in loads:
+    for load in loads[:2]:
+        load.start()
+
+    @pl.when(is_first)
+    def _():
+        for i in range(freq_count - 1):
+            greet(i, 0)
+
+    neighbours = 0
+    for i in (-2, -1, 1, 2):
+        neighbours += in_sky(i).astype(jnp.int32)
+
+        @pl.when(in_sky(i))
+        def _():
+            pl.semaphore_signal(barrier, inc=1, device_id={"sky": sky + i}, device_id_type=MESH)
+
+    for load in loads[2:]:
         load.start()
     pl.semaphore_wait(barrier, cut - is_first.astype(jnp.int32) + neighbours)
 
@@ -399,10 +406,6 @@
     def _():
         for i in range(cut):
             announce(i, 0)
-
-    loads[0].wait()
-    loads[1].wait()
-    fill_tx(cube, free, tx)
 
     def exchange(peer):
         return pltpu.make_async_remote_copy(
@@ -436,9 +439,9 @@
     def to_hub(peer):
         return pltpu.make_async_remote_copy(
             src_ref=tx.at[peer],
-            dst_ref=passing.at[freq - cut],
+            dst_ref=passing.at[freq - origin],
             send_sem=send_sem.at[peer],
-            recv_sem=hub_recv.at[freq - cut],
+            recv_sem=hub_recv.at[freq - origin],
             device_id={"freq": hub_of(peer)},
             device_id_type=MESH,
         )
@@ -446,9 +449,9 @@
     def from_hub(slot):
         return pltpu.make_async_remote_copy(
             src_ref=passing.at[slot],
-            dst_ref=rx.at[cut + slot],
+            dst_ref=rx.at[origin + slot],
             send_sem=hub_send.at[slot],
-            recv_sem=recv_sem.at[cut + slot],
+            recv_sem=recv_sem.at[origin + slot],
             device_id={"freq": end + 2 * (hubs - freq // 2) + lax.rem(freq, 2)},
             device_id_type=MESH,
         )
@@ -459,7 +462,7 @@
             dst_ref=passing.at[slot],
             send_sem=hub_send.at[slot],
             recv_sem=hub_recv.at[slot],
-            device_id={"freq": cut + slot},
+            device_id={"freq": origin + slot},
             device_id_type=MESH,
         )
 
@@ -478,8 +481,9 @@
         def _():
             arrival(i).wait_send()
 
-    for i in range(cut):
-        send(i)
+    loads[0].wait()
+    loads[1].wait()
+    fill_tx(cube, free, tx, cut, send)
 
     @pl.when(is_source)
     def _():
@@ -523,7 +527,7 @@
 
     @pl.when(is_hub)
     def _():
-        for slot in range(middle - cut):
+        for slot in range(middle - origin):
             at_hub(slot).wait_recv()
             from_hub(slot).start()
 
@@ -565,7 +569,7 @@
 
     @pl.when(is_hub)
     def _():
-        for slot in range(middle - cut):
+        for slot in range(middle - origin):
             from_hub(slot).wait_send()
 
     for i, halo in halos:
@@ -620,9 +624,9 @@
         pltpu.SemaphoreType.DMA((4,)),
         pltpu.SemaphoreType.REGULAR,
         pltpu.SemaphoreType.REGULAR,
-        pltpu.VMEM((freq_count // 4, chans * rows, LANES), BF16),
-        pltpu.SemaphoreType.DMA((freq_count // 4,)),
-        pltpu.SemaphoreType.DMA((freq_count // 4,)),
+        pltpu.VMEM((freq_count // 2, chans * rows, LANES), BF16),
+        pltpu.SemaphoreType.DMA((freq_count // 2,)),
+        pltpu.SemaphoreType.DMA((freq_count // 2,)),
     ]
     shape = (freq_count, sky_count, rows * sky_count, cols)
     result = pl.pallas_call(

time: 31.6 us -> 31.6 us (level)
  the two profiles are of different devices: /device:TPU:459 before, /device:TPU:1 now
where the time goes in v6:
time: 31.6 us; the launch traced here: 31.1 us
  Pallas kernels  29.3 us (93%)
  local copies, waits for them, and re-layouts  1.22 us (4%)
  between operations  0.64 us (2%)
    pallas_call x1, Pallas kernels, on_device(): pl.pallas_call(functools.partial(body, shape), out_shape=pltpu.VMEM((ANCH...  29.3 us

profile of v6, /device:TPU:1, one launch (start us, length us, event | category | flops | bytes accessed | tf_op | source)
XLA Modules:
  0.0 31.1 jit_solution(10733107686719952350)
XLA Ops:
  0.6 29.3 %shard_map.86 = f32[9,5,2,64]{3,2,1,0:T(2,128)S(1)} custom-call(bf16[2,2,2048]{2,1,0:T(2,128)(2,1)} %cube_hbm.1, s32[1,2]{1,0:T(1,128)} %bitcast.11, bf16[9,3,32]{2,1,0:T(4,128)(2,1)} %bitcast.10, bf16[27,32,32]{2,1,0:T(8,128)(2,1)} %bitcast.9, bf16[3,3,64,256]{3,2,1,0:T(8,128)(2,1)} %proposal_hbm.1, bf16[9,256]{1,0:T(8,128)(2,1)} %score_hbm.1, ...), custom_call_target="tpu_custom_call" | custom-call | tf_op jit(solution)/shard_map/pallas_call | solution.py:632
  29.9 0.6 %slice_bitcast_fusion = f32[9,2,64]{2,1,0:T(2,128)} fusion(f32[9,5,2,64]{3,2,1,0:T(2,128)S(1)} %shard_map.86), kind=kLoop, calls=%fused_computation | loop fusion | bytes 9216 | tf_op jit(solution)/shard_map/squeeze | solution.py:642
  30.5 0.6 %slice.7 = f32[9,4,2,64]{3,2,1,0:T(2,128)} slice(f32[9,5,2,64]{3,2,1,0:T(2,128)S(1)} %shard_map.86), slice={[0:9], [1:5], [0:2], [0:64]} | slice | bytes 36864 | tf_op jit(solution)/shard_map/slice | solution.py:642

commit v7 on v6

--- a/solution.py
+++ b/solution.py
@@ -25,7 +25,7 @@
 LATE = 4
 WINDOW = 8
 WINDOWS = CHANS // 2 // WINDOW
-GROUP = 4
+GROUP = 2
 NT = (((1,), (1,)), ((), ()))
 
 
@@ -602,7 +602,7 @@
         pltpu.VMEM((freq_count, chans * rows, LANES), BF16),
         pltpu.VMEM((freq_count, chans * rows, LANES), BF16),
         pltpu.VMEM((8, CHANS, LANES), BF16),
-        pltpu.VMEM((2 * CHANS, LANES), F32),
+        pltpu.VMEM((2 * CHANS + 8, LANES), F32),
         pltpu.VMEM((4 * CHANS + 48, LANES), F32),
         pltpu.VMEM((8 * CHANS + 80, LANES), F32),
         pltpu.VMEM((3, 4 * CHANS + 48, LANES), BF16),

time: 31.6 us -> 31.6 us (level)
  no operation moved by 1% of the time
where the time goes in v7:
time: 31.6 us; the launch traced here: 31.1 us
  Pallas kernels  29.3 us (93%)
  local copies, waits for them, and re-layouts  1.22 us (4%)
  between operations  0.64 us (2%)
    pallas_call x1, Pallas kernels, on_device(): pl.pallas_call(functools.partial(body, shape), out_shape=pltpu.VMEM((ANCH...  29.3 us

profile of v7, /device:TPU:1, one launch (start us, length us, event | category | flops | bytes accessed | tf_op | source)
XLA Modules:
  0.0 31.1 jit_solution(15650420697550204734)
XLA Ops:
  0.6 29.3 %shard_map.86 = f32[9,5,2,64]{3,2,1,0:T(2,128)S(1)} custom-call(bf16[2,2,2048]{2,1,0:T(2,128)(2,1)} %cube_hbm.1, s32[1,2]{1,0:T(1,128)} %bitcast.11, bf16[9,3,32]{2,1,0:T(4,128)(2,1)} %bitcast.10, bf16[27,32,32]{2,1,0:T(8,128)(2,1)} %bitcast.9, bf16[3,3,64,256]{3,2,1,0:T(8,128)(2,1)} %proposal_hbm.1, bf16[9,256]{1,0:T(8,128)(2,1)} %score_hbm.1, ...), custom_call_target="tpu_custom_call" | custom-call | tf_op jit(solution)/shard_map/pallas_call | solution.py:632
  29.9 0.6 %slice_bitcast_fusion = f32[9,2,64]{2,1,0:T(2,128)} fusion(f32[9,5,2,64]{3,2,1,0:T(2,128)S(1)} %shard_map.86), kind=kLoop, calls=%fused_computation | loop fusion | bytes 9216 | tf_op jit(solution)/shard_map/squeeze | solution.py:642
  30.5 0.6 %slice.7 = f32[9,4,2,64]{3,2,1,0:T(2,128)} slice(f32[9,5,2,64]{3,2,1,0:T(2,128)S(1)} %shard_map.86), slice={[0:9], [1:5], [0:2], [0:64]} | slice | bytes 36864 | tf_op jit(solution)/shard_map/slice | solution.py:642

commit v8 on v7

--- a/solution.py
+++ b/solution.py
@@ -347,7 +347,7 @@
     sky = lax.axis_index("sky")
     odd = lax.rem(sky, 2) == 1
     barrier = pltpu.get_barrier_semaphore()
-    cut = max(2, freq_count * 7 // 16 // 2 * 2)
+    cut = max(2, freq_count * 8 // 16 // 2 * 2)
     is_first = freq < cut
     middle = freq_count * 11 // 16
     end = freq_count * 3 // 4

time: 31.6 us -> 31.6 us (level)
  no operation moved by 1% of the time
where the time goes in v8:
time: 31.6 us; the launch traced here: 31.1 us
  Pallas kernels  29.3 us (93%)
  local copies, waits for them, and re-layouts  1.22 us (4%)
  between operations  0.64 us (2%)
    pallas_call x1, Pallas kernels, on_device(): pl.pallas_call(functools.partial(body, shape), out_shape=pltpu.VMEM((ANCH...  29.3 us

profile of v8, /device:TPU:1, one launch (start us, length us, event | category | flops | bytes accessed | tf_op | source)
XLA Modules:
  0.0 31.1 jit_solution(2982397625947350755)
XLA Ops:
  0.6 29.3 %shard_map.86 = f32[9,5,2,64]{3,2,1,0:T(2,128)S(1)} custom-call(bf16[2,2,2048]{2,1,0:T(2,128)(2,1)} %cube_hbm.1, s32[1,2]{1,0:T(1,128)} %bitcast.11, bf16[9,3,32]{2,1,0:T(4,128)(2,1)} %bitcast.10, bf16[27,32,32]{2,1,0:T(8,128)(2,1)} %bitcast.9, bf16[3,3,64,256]{3,2,1,0:T(8,128)(2,1)} %proposal_hbm.1, bf16[9,256]{1,0:T(8,128)(2,1)} %score_hbm.1, ...), custom_call_target="tpu_custom_call" | custom-call | tf_op jit(solution)/shard_map/pallas_call | solution.py:632
  29.9 0.6 %slice_bitcast_fusion = f32[9,2,64]{2,1,0:T(2,128)} fusion(f32[9,5,2,64]{3,2,1,0:T(2,128)S(1)} %shard_map.86), kind=kLoop, calls=%fused_computation | loop fusion | bytes 9216 | tf_op jit(solution)/shard_map/squeeze | solution.py:642
  30.5 0.6 %slice.7 = f32[9,4,2,64]{3,2,1,0:T(2,128)} slice(f32[9,5,2,64]{3,2,1,0:T(2,128)S(1)} %shard_map.86), slice={[0:9], [1:5], [0:2], [0:64]} | slice | bytes 36864 | tf_op jit(solution)/shard_map/slice | solution.py:642
